TPU v7x, 512 devices: a whole 4x8x8 slice. The times are simulated.
512 devices in a mesh: region: 64 (over x, z, core), lane: 8 (over y).
Axes of the slice: x: 4, y: 8, z: 8, core: 2. Of those that a mesh axis runs over, the one named last changes fastest.
Arguments:
- init_disp: float32 [3, 524288], P(None, 'region'), may hold values from -0.9 to 1.2
- init_vel: float32 [3, 524288], P(None, 'region'), may hold values from -3 to 3
- mass: float32 [524288], P('region'), may hold values from 0.5 to 2
- contact: float32 [524288], P('region'), may hold values from 0.1 to 16, as said below
- modulus: float32 [32768, 16], P(('region', 'lane')), may hold values from 0.5 to 3
- stiffness: float32 [24, 24], replicated, may hold values from -0.5 to 1.5, as said below
- levels: int32 [32768], P(('region', 'lane')), may hold values from 1 to 8, as said below
- windows: int32 [32768], P(('region', 'lane')), may hold values from 0 to 64
- conn: int32 [32768, 128], P(('region', 'lane')), may hold values from 0 to 255
Outputs:
- displacement: float32 [3, 524288], P(None, 'region')
- velocity: float32 [3, 524288], P(None, 'region')
- reaction: float32 [8], replicated
Inputs may be any that keep to these rules, and one draw needn't show every extreme that they name: `levels`: each entry is 1, 2, 4 or 8. The number of 1s among the 64 blocks of one device differs between devices and equals 64 on some device. `contact`: positive weights. `stiffness`: Symmetric.
All inputs are finite; a program needn't handle non-finite values.
Results may differ from a plain program's by a relative error of at most 0.0003.
Values sent between devices are 32-bit elements; how exact they have to be, the bound alone decides.
A program may use at most 64 MiB of HBM per device.

v0:
```python
import jax
import jax.numpy as jnp
from jax import lax
from jax.sharding import PartitionSpec as P

NB = 128
SUBSTEPS = 8


time_step = 0.05
contact_stiffness = 1.0
hardening = 2.0
impactor_ratio = 0.05
start_gap = 1.0
start_speed = 1.0
group_size = 8


def with_halo(array, sides, width):
    for axis, dim in sides:
        count, length = (lax.axis_size(axis), array.shape[dim])
        up = [(i, (i + 1) % count) for i in range(count)]
        down = [(j, i) for i, j in up]
        last = lax.slice_in_dim(array, length - width, length, axis=dim)
        initial = lax.slice_in_dim(array, 0, width, axis=dim)
        before = lax.ppermute(last, axis, up)
        after = lax.ppermute(initial, axis, down)
        array = jnp.concatenate([before, array, after], axis=dim)
    return array


def element_forces(slot_disp, block_modulus, stiffness):
    count = slot_disp.shape[0]
    elements = block_modulus.shape[1]
    vectors = (
        slot_disp.reshape(count, 3, elements, 8).transpose(0, 2, 1, 3).reshape(count, elements, 24)
    )
    strain = jnp.einsum("bek,jk->bej", vectors, stiffness, precision=lax.Precision.HIGHEST)
    result = block_modulus[:, :, None] * (strain + hardening * strain * strain * strain)
    return (
        result.reshape(count, elements, 3, 8).transpose(0, 2, 1, 3).reshape(count, 3, elements * 8)
    )


def on_device(init_disp, init_vel, mass, contact, modulus, stiffness, levels, windows, conn):
    region_count = lax.axis_size("region")
    node_region = init_disp.shape[1]
    slot_count = conn.shape[1]
    block_rows = NB
    node_total = node_region * region_count
    impactor_mass = impactor_ratio * node_total
    extended_blocks = node_region // block_rows + 2
    block_order = jnp.argsort(levels, stable=True)
    conn = conn[block_order]
    windows = windows[block_order]
    levels = levels[block_order]
    modulus = modulus[block_order]
    level_slot = (
        (levels >= 2).astype(jnp.int32)
        + (levels >= 4).astype(jnp.int32)
        + (levels >= 8).astype(jnp.int32)
    )
    level_force = jnp.zeros((4, 3, extended_blocks, block_rows), jnp.float32)
    disp_full = init_disp
    disp_state = init_disp
    vel_state = init_vel
    gap_now = jnp.float32(start_gap)
    speed = jnp.float32(start_speed)
    history = []
    slot_iota = lax.broadcasted_iota(jnp.int32, (group_size, 2 * block_rows, slot_count), 1)
    for substep in range(SUBSTEPS):
        top_level = SUBSTEPS if substep == 0 else min(substep & -substep, SUBSTEPS)
        top_index = top_level.bit_length() - 1
        active_count = jnp.sum((levels <= top_level).astype(jnp.int32))
        level_force = level_force.at[: top_index + 1].set(0.0)
        disp_ext = with_halo(disp_full, (("region", 1),), block_rows)

        def one_group(group_index, totals):
            offset = group_index * group_size
            conn_group = lax.dynamic_slice_in_dim(conn, offset, group_size, 0)
            window_group = lax.dynamic_slice_in_dim(windows, offset, group_size, 0)
            level_group = lax.dynamic_slice_in_dim(level_slot, offset, group_size, 0)
            modulus_group = lax.dynamic_slice_in_dim(modulus, offset, group_size, 0)
            valid = offset + jnp.arange(group_size, dtype=jnp.int32) < active_count
            window_disp = jax.vmap(
                lambda first_block: lax.dynamic_slice_in_dim(
                    disp_ext, first_block * block_rows, 2 * block_rows, 1
                )
            )(window_group)
            onehot = (slot_iota == conn_group[:, None, :]).astype(jnp.float32)
            slot_disp = jnp.einsum(
                "gcw,gws->gcs", window_disp, onehot, precision=lax.Precision.HIGHEST
            )
            slot_force = element_forces(slot_disp, modulus_group, stiffness)
            slot_force = jnp.where(valid[:, None, None], slot_force, 0.0)
            window_force = jnp.einsum(
                "gcs,gws->gcw", slot_force, onehot, precision=lax.Precision.HIGHEST
            )
            window_force = window_force.reshape(group_size, 3, 2, block_rows)
            totals = totals.at[level_group, :, window_group].add(window_force[:, :, 0])
            totals = totals.at[level_group, :, window_group + 1].add(window_force[:, :, 1])
            return totals

        group_total = (active_count + group_size - 1) // group_size
        level_force = lax.fori_loop(0, group_total, one_group, level_force)
        force_ext = jnp.sum(level_force, axis=0).reshape(3, extended_blocks * block_rows)
        outer_rims = jnp.concatenate(
            (force_ext[:, :block_rows], force_ext[:, -block_rows:]), axis=1
        )
        rim_terms = with_halo(outer_rims, (("region", 1),), block_rows)
        partial_force = force_ext[:, block_rows:-block_rows]
        partial_force = partial_force.at[:, :block_rows].add(rim_terms[:, :block_rows])
        partial_force = partial_force.at[:, -block_rows:].add(rim_terms[:, -block_rows:])
        force = lax.psum(partial_force, "lane")
        disp_state = disp_full
        gap = gap_now - disp_state[0]
        total = lax.psum(jnp.sum(contact * gap), "region")
        history.append(total / node_total)
        push = jnp.zeros_like(force).at[0].set(contact_stiffness * contact * gap)
        accel = (push - force) / mass[None, :]
        vel_state = vel_state + time_step * accel
        disp_state = disp_state + time_step * vel_state
        speed = speed - time_step * contact_stiffness * total / impactor_mass
        gap_now = gap_now + time_step * speed
        disp_full = disp_state
    return (disp_full, vel_state, jnp.stack(history))


def solution(mesh):
    in_specs = (
        P(None, "region"),
        P(None, "region"),
        P("region"),
        P("region"),
        P(("region", "lane"), None),
        P(),
        P(("region", "lane")),
        P(("region", "lane")),
        P(("region", "lane"), None),
    )
    out_specs = (P(None, "region"), P(None, "region"), P())
    return jax.shard_map(
        on_device, mesh=mesh, in_specs=in_specs, out_specs=out_specs, check_vma=False
    )
```

profile of v0, /device:TPU:1, one launch (start us, length us, event | category | flops | bytes accessed | tf_op | source)
XLA Modules:
  0.0 2183.8 jit_solution(9804989991320243349)
XLA Ops:
  7.9 8.8 collective-permute-start.1
  26.6 116.3 %while.163 = (s32[]{:T(128)}, f32[4,3,66,128]{3,1,2,0:T(4,128)S(1)}, s32[]{:T(128)}, s32[64]{0:T(128)S(1)}, s32[64]{0:T(128)S(1)}, /*index=5*/s32[]{:T(128)}, f3...) while((s32[]{:T(128)}, f32[4,3,66,128]{3,1,2,0:T(4,128)S(1)}, ...), condition=%wide.region_5.6_spmd.clone, body=%wide.region_2.5_spmd.clone.sunk | while | flops 20308224 | bytes 569896 | solution.py:105
  26.8 9.8 while.178
  41.4 9.8 while.178
  55.9 9.8 while.178
  70.5 9.8 while.178
  85.0 9.8 while.178
  99.5 9.8 while.178
  114.1 9.8 while.178
  128.6 9.8 while.178
  155.2 129.4 %psum.113 = f32[]{:T(128)} all-reduce(f32[]{:T(128)} %get-tuple-element.2038), channel_id=1, replica_groups=mesh['region'=64,'lane'=8] {'region'}, use_global_device_ids=true, to_apply=%region_10.11 | all-reduce | flops 1 | bytes 8 | tf_op jit(solution)/shard_map/psum | solution.py:117
  299.0 48.3 %while.165 = (s32[]{:T(128)}, f32[4,3,66,128]{3,1,2,0:T(4,128)S(1)}, s32[]{:T(128)}, s32[64]{0:T(128)S(1)}, s32[64]{0:T(128)S(1)}, /*index=5*/s32[]{:T(128)}, f3...) while((s32[]{:T(128)}, f32[4,3,66,128]{3,1,2,0:T(4,128)S(1)}, ...), condition=%wide.region_15.16_spmd.clone, body=%wide.region_12.15_spmd.clone.sunk | while | flops 20308224 | bytes 569896 | solution.py:105
  299.2 11.4 while.179
  315.3 11.4 while.179
  331.4 11.4 while.179
  347.4 36.0 %collective-permute-start.6 = (f32[3,128]{1,0:T(4,128)S(1)}, f32[3,128]{1,0:T(4,128)S(1)}, u32[]{:S(2)}, u32[]{:S(2)}) collective-permute-start(f32[3,128]{1,0:T(4,128)S(1)} %get-tuple-element.2085), channel_id=1, source_target_pairs={{0,8},{8,16},{16,24},{24,32},{32,40},{40,48},{48,56},{56,64},{64,7... | collective-permute-start | bytes 4616 | tf_op jit(solution)/shard_map/ppermute | solution.py:26
  383.5 37.6 %collective-permute-start.7 = (f32[3,128]{1,0:T(4,128)S(1)}, f32[3,128]{1,0:T(4,128)S(1)}, u32[]{:S(2)}, u32[]{:S(2)}) collective-permute-start(f32[3,128]{1,0:T(4,128)S(1)} %get-tuple-element.2084), channel_id=1, source_target_pairs={{8,0},{16,8},{24,16},{32,24},{40,32},{48,40},{56,48},{64,56},{72,6... | collective-permute-start | bytes 4616 | tf_op jit(solution)/shard_map/ppermute | solution.py:27
  423.3 129.5 %psum.115 = f32[]{:T(128)} all-reduce(f32[]{:T(128)} %get-tuple-element.2034), channel_id=1, replica_groups=mesh['region'=64,'lane'=8] {'region'}, use_global_device_ids=true, to_apply=%region_19.20 | all-reduce | flops 1 | bytes 8 | tf_op jit(solution)/shard_map/psum | solution.py:117
  565.2 64.0 %while.167 = (s32[]{:T(128)}, f32[4,3,66,128]{3,1,2,0:T(4,128)S(1)}, s32[]{:T(128)}, s32[64]{0:T(128)S(1)}, s32[64]{0:T(128)S(1)}, /*index=5*/s32[]{:T(128)}, f3...) while((s32[]{:T(128)}, f32[4,3,66,128]{3,1,2,0:T(4,128)S(1)}, ...), condition=%wide.region_24.25_spmd.clone, body=%wide.region_21.24_spmd.clone.sunk | while | flops 20308224 | bytes 569896 | solution.py:105
  565.5 11.3 while.180
  581.5 11.3 while.180
  597.5 11.3 while.180
  613.5 11.3 while.180
  629.4 35.8 %collective-permute-start.10 = (f32[3,128]{1,0:T(4,128)S(1)}, f32[3,128]{1,0:T(4,128)S(1)}, u32[]{:S(2)}, u32[]{:S(2)}) collective-permute-start(f32[3,128]{1,0:T(4,128)S(1)} %get-tuple-element.2083), channel_id=1, source_target_pairs={{0,8},{8,16},{16,24},{24,32},{32,40},{40,48},{48,56},{56,64},{64,7... | collective-permute-start | bytes 4616 | tf_op jit(solution)/shard_map/ppermute | solution.py:26
  665.3 37.3 %collective-permute-start.11 = (f32[3,128]{1,0:T(4,128)S(1)}, f32[3,128]{1,0:T(4,128)S(1)}, u32[]{:S(2)}, u32[]{:S(2)}) collective-permute-start(f32[3,128]{1,0:T(4,128)S(1)} %get-tuple-element.2082), channel_id=1, source_target_pairs={{8,0},{16,8},{24,16},{32,24},{40,32},{48,40},{56,48},{64,56},{72,6... | collective-permute-start | bytes 4616 | tf_op jit(solution)/shard_map/ppermute | solution.py:27
  704.8 129.5 %psum.117 = f32[]{:T(128)} all-reduce(f32[]{:T(128)} %get-tuple-element.2032), channel_id=1, replica_groups=mesh['region'=64,'lane'=8] {'region'}, use_global_device_ids=true, to_apply=%region_28.29 | all-reduce | flops 1 | bytes 8 | tf_op jit(solution)/shard_map/psum | solution.py:117
  846.7 49.0 %while.169 = (s32[]{:T(128)}, f32[4,3,66,128]{3,1,2,0:T(4,128)S(1)}, s32[]{:T(128)}, s32[64]{0:T(128)S(1)}, s32[64]{0:T(128)S(1)}, /*index=5*/s32[]{:T(128)}, f3...) while((s32[]{:T(128)}, f32[4,3,66,128]{3,1,2,0:T(4,128)S(1)}, ...), condition=%wide.region_32.33_spmd.clone, body=%wide.region_29.32_spmd.clone.sunk | while | flops 20308224 | bytes 569896 | solution.py:105
  847.1 11.5 while.181
  863.3 11.5 while.181
  879.6 11.5 while.181
  895.8 36.3 %collective-permute-start.14 = (f32[3,128]{1,0:T(4,128)S(1)}, f32[3,128]{1,0:T(4,128)S(1)}, u32[]{:S(2)}, u32[]{:S(2)}) collective-permute-start(f32[3,128]{1,0:T(4,128)S(1)} %get-tuple-element.2081), channel_id=1, source_target_pairs={{0,8},{8,16},{16,24},{24,32},{32,40},{40,48},{48,56},{56,64},{64,7... | collective-permute-start | bytes 4616 | tf_op jit(solution)/shard_map/ppermute | solution.py:26
  932.2 37.9 %collective-permute-start.15 = (f32[3,128]{1,0:T(4,128)S(1)}, f32[3,128]{1,0:T(4,128)S(1)}, u32[]{:S(2)}, u32[]{:S(2)}) collective-permute-start(f32[3,128]{1,0:T(4,128)S(1)} %get-tuple-element.2080), channel_id=1, source_target_pairs={{8,0},{16,8},{24,16},{32,24},{40,32},{48,40},{56,48},{64,56},{72,6... | collective-permute-start | bytes 4616 | tf_op jit(solution)/shard_map/ppermute | solution.py:27
  972.3 129.5 %psum.119 = f32[]{:T(128)} all-reduce(f32[]{:T(128)} %get-tuple-element.2028), channel_id=1, replica_groups=mesh['region'=64,'lane'=8] {'region'}, use_global_device_ids=true, to_apply=%region_36.37 | all-reduce | flops 1 | bytes 8 | tf_op jit(solution)/shard_map/psum | solution.py:117
  1114.3 76.0 %while.171 = (s32[]{:T(128)}, f32[4,3,66,128]{3,1,2,0:T(4,128)S(1)}, s32[]{:T(128)}, s32[64]{0:T(128)S(1)}, s32[64]{0:T(128)S(1)}, /*index=5*/s32[]{:T(128)}, f3...) while((s32[]{:T(128)}, f32[4,3,66,128]{3,1,2,0:T(4,128)S(1)}, ...), condition=%wide.region_41.42_spmd.clone, body=%wide.region_38.41_spmd.clone.sunk | while | flops 20308224 | bytes 569896 | solution.py:105
  1114.5 10.5 while.182
  1129.7 10.5 while.182
  1144.9 10.5 while.182
  1160.1 10.5 while.182
  1175.3 10.5 while.182
  1190.4 19.0 collective-permute-start.18
  1209.5 35.7 %collective-permute-start.19 = (f32[3,128]{1,0:T(4,128)S(1)}, f32[3,128]{1,0:T(4,128)S(1)}, u32[]{:S(2)}, u32[]{:S(2)}) collective-permute-start(f32[3,128]{1,0:T(4,128)S(1)} %get-tuple-element.2078), channel_id=1, source_target_pairs={{8,0},{16,8},{24,16},{32,24},{40,32},{48,40},{56,48},{64,56},{72,6... | collective-permute-start | bytes 4616 | tf_op jit(solution)/shard_map/ppermute | solution.py:27
  1247.3 129.6 %psum.121 = f32[]{:T(128)} all-reduce(f32[]{:T(128)} %get-tuple-element.2026), channel_id=1, replica_groups=mesh['region'=64,'lane'=8] {'region'}, use_global_device_ids=true, to_apply=%region_45.46 | all-reduce | flops 1 | bytes 8 | tf_op jit(solution)/shard_map/psum | solution.py:117
  1389.3 46.2 %while.173 = (s32[]{:T(128)}, f32[4,3,66,128]{3,1,2,0:T(4,128)S(1)}, s32[]{:T(128)}, s32[64]{0:T(128)S(1)}, s32[64]{0:T(128)S(1)}, /*index=5*/s32[]{:T(128)}, f3...) while((s32[]{:T(128)}, f32[4,3,66,128]{3,1,2,0:T(4,128)S(1)}, ...), condition=%wide.region_49.50_spmd.clone, body=%wide.region_46.49_spmd.clone.sunk | while | flops 20308224 | bytes 569896 | solution.py:105
  1389.5 10.7 while.183
  1404.9 10.7 while.183
  1420.3 10.7 while.183
  1435.6 34.6 %collective-permute-start.22 = (f32[3,128]{1,0:T(4,128)S(1)}, f32[3,128]{1,0:T(4,128)S(1)}, u32[]{:S(2)}, u32[]{:S(2)}) collective-permute-start(f32[3,128]{1,0:T(4,128)S(1)} %get-tuple-element.2077), channel_id=1, source_target_pairs={{0,8},{8,16},{16,24},{24,32},{32,40},{40,48},{48,56},{56,64},{64,7... | collective-permute-start | bytes 4616 | tf_op jit(solution)/shard_map/ppermute | solution.py:26
  1470.3 36.2 %collective-permute-start.23 = (f32[3,128]{1,0:T(4,128)S(1)}, f32[3,128]{1,0:T(4,128)S(1)}, u32[]{:S(2)}, u32[]{:S(2)}) collective-permute-start(f32[3,128]{1,0:T(4,128)S(1)} %get-tuple-element.2076), channel_id=1, source_target_pairs={{8,0},{16,8},{24,16},{32,24},{40,32},{48,40},{56,48},{64,56},{72,6... | collective-permute-start | bytes 4616 | tf_op jit(solution)/shard_map/ppermute | solution.py:27
  1508.6 129.5 %psum.123 = f32[]{:T(128)} all-reduce(f32[]{:T(128)} %get-tuple-element.2022), channel_id=1, replica_groups=mesh['region'=64,'lane'=8] {'region'}, use_global_device_ids=true, to_apply=%region_53.54 | all-reduce | flops 1 | bytes 8 | tf_op jit(solution)/shard_map/psum | solution.py:117
  1650.5 60.9 %while.175 = (s32[]{:T(128)}, f32[4,3,66,128]{3,1,2,0:T(4,128)S(1)}, s32[]{:T(128)}, s32[64]{0:T(128)S(1)}, s32[64]{0:T(128)S(1)}, /*index=5*/s32[]{:T(128)}, f3...) while((s32[]{:T(128)}, f32[4,3,66,128]{3,1,2,0:T(4,128)S(1)}, ...), condition=%wide.region_57.58_spmd.clone, body=%wide.region_54.57_spmd.clone.sunk | while | flops 20308224 | bytes 569896 | solution.py:105
  1650.7 10.5 while.184
  1665.9 10.5 while.184
  1681.1 10.5 while.184
  1696.4 10.5 while.184
  1711.5 34.2 %collective-permute-start.26 = (f32[3,128]{1,0:T(4,128)S(1)}, f32[3,128]{1,0:T(4,128)S(1)}, u32[]{:S(2)}, u32[]{:S(2)}) collective-permute-start(f32[3,128]{1,0:T(4,128)S(1)} %get-tuple-element.2075), channel_id=1, source_target_pairs={{0,8},{8,16},{16,24},{24,32},{32,40},{40,48},{48,56},{56,64},{64,7... | collective-permute-start | bytes 4616 | tf_op jit(solution)/shard_map/ppermute | solution.py:26
  1745.8 35.7 %collective-permute-start.27 = (f32[3,128]{1,0:T(4,128)S(1)}, f32[3,128]{1,0:T(4,128)S(1)}, u32[]{:S(2)}, u32[]{:S(2)}) collective-permute-start(f32[3,128]{1,0:T(4,128)S(1)} %get-tuple-element.2074), channel_id=1, source_target_pairs={{8,0},{16,8},{24,16},{32,24},{40,32},{48,40},{56,48},{64,56},{72,6... | collective-permute-start | bytes 4616 | tf_op jit(solution)/shard_map/ppermute | solution.py:27
  1783.7 129.5 %psum.125 = f32[]{:T(128)} all-reduce(f32[]{:T(128)} %get-tuple-element.2020), channel_id=1, replica_groups=mesh['region'=64,'lane'=8] {'region'}, use_global_device_ids=true, to_apply=%region_61.62 | all-reduce | flops 1 | bytes 8 | tf_op jit(solution)/shard_map/psum | solution.py:117
  1925.5 46.1 %while.177 = (s32[]{:T(128)}, f32[4,3,66,128]{3,1,2,0:T(4,128)S(1)}, s32[]{:T(128)}, s32[64]{0:T(128)S(1)}, s32[64]{0:T(128)S(1)}, /*index=5*/s32[]{:T(128)}, f3...) while((s32[]{:T(128)}, f32[4,3,66,128]{3,1,2,0:T(4,128)S(1)}, ...), condition=%wide.region_65.66_spmd.clone, body=%wide.region_62.65_spmd.clone.sunk | while | flops 20308224 | bytes 569896 | solution.py:105
  1925.7 10.6 while.185
  1941.1 10.6 while.185
  1956.5 10.6 while.185
  1971.8 34.5 %collective-permute-start.30 = (f32[3,128]{1,0:T(4,128)S(1)}, f32[3,128]{1,0:T(4,128)S(1)}, u32[]{:S(2)}, u32[]{:S(2)}) collective-permute-start(f32[3,128]{1,0:T(4,128)S(1)} %get-tuple-element.2073), channel_id=1, source_target_pairs={{0,8},{8,16},{16,24},{24,32},{32,40},{40,48},{48,56},{56,64},{64,7... | collective-permute-start | bytes 4616 | tf_op jit(solution)/shard_map/ppermute | solution.py:26
  2006.3 36.0 %collective-permute-start.31 = (f32[3,128]{1,0:T(4,128)S(1)}, f32[3,128]{1,0:T(4,128)S(1)}, u32[]{:S(2)}, u32[]{:S(2)}) collective-permute-start(f32[3,128]{1,0:T(4,128)S(1)} %get-tuple-element.2072), channel_id=1, source_target_pairs={{8,0},{16,8},{24,16},{32,24},{40,32},{48,40},{56,48},{64,56},{72,6... | collective-permute-start | bytes 4616 | tf_op jit(solution)/shard_map/ppermute | solution.py:27
  2044.4 129.6 %psum.127 = f32[]{:T(128)} all-reduce(f32[]{:T(128)} %get-tuple-element.2016), channel_id=1, replica_groups=mesh['region'=64,'lane'=8] {'region'}, use_global_device_ids=true, to_apply=%region_69.70 | all-reduce | flops 1 | bytes 8 | tf_op jit(solution)/shard_map/psum | solution.py:117
  (1832 shorter events, 623.5 us)
Async XLA Ops:
  7.2 17.8 copy-start
  7.2 280.0 %all-reduce.25.cloned.1.call-start = ((), (), s32[]{:S(2)}) async-start(), calls=%async_computation | async-start | bytes 262144 | tf_op jit(solution)/shard_map/psum | solution.py:114
  7.9 17.7 collective-permute-start.1
  16.7 2.0 copy-start.1
  16.7 8.9 collective-permute-start
  22.9 0.7 copy-start.2
  23.5 0.8 copy-start.20
  25.0 0.9 copy-start.6
  25.9 0.7 copy-start.3
  143.1 9.9 collective-permute-start.2
  145.8 8.0 collective-permute-start.3
  153.8 0.7 copy-start.8
  153.8 0.8 copy-start.5
  154.5 132.7 %copy-start.15 = (f32[3,8192]{1,0:T(4,128)S(1)}, f32[3,8192]{1,0:T(4,128)}, u32[]{:S(2)}) copy-start(f32[3,8192]{1,0:T(4,128)} %param.95) | copy-start | bytes 294916
  154.5 399.0 %all-reduce.27.cloned.1.call-start = ((), (), s32[]{:S(2)}) async-start(), calls=%async_computation.1 | async-start | bytes 262144 | tf_op jit(solution)/shard_map/psum | solution.py:114
  286.5 0.8 copy-start.4
  288.3 9.5 collective-permute-start.5
  295.9 3.1 collective-permute-start.4
  347.4 73.7 %collective-permute-start.6 = (f32[3,128]{1,0:T(4,128)S(1)}, f32[3,128]{1,0:T(4,128)S(1)}, u32[]{:S(2)}, u32[]{:S(2)}) collective-permute-start(f32[3,128]{1,0:T(4,128)S(1)} %get-tuple-element.2085), channel_id=1, source_target_pairs={{0,8},{8,16},{16,24},{24,32},{32,40},{40,48},{48,56},{56,64},{64,7... | collective-permute-start | bytes 4616 | tf_op jit(solution)/shard_map/ppermute | solution.py:26
  383.4 170.1 %copy-start.16 = (f32[3,8192]{1,0:T(4,128)S(1)}, f32[3,8192]{1,0:T(4,128)}, u32[]{:S(2)}) copy-start(f32[3,8192]{1,0:T(4,128)} %all-reduce.25.cloned.1.call-done) | copy-start | bytes 294916
  383.5 38.4 %collective-permute-start.7 = (f32[3,128]{1,0:T(4,128)S(1)}, f32[3,128]{1,0:T(4,128)S(1)}, u32[]{:S(2)}, u32[]{:S(2)}) collective-permute-start(f32[3,128]{1,0:T(4,128)S(1)} %get-tuple-element.2084), channel_id=1, source_target_pairs={{8,0},{16,8},{24,16},{32,24},{40,32},{48,40},{56,48},{64,56},{72,6... | collective-permute-start | bytes 4616 | tf_op jit(solution)/shard_map/ppermute | solution.py:27
  421.9 0.7 copy-start.9
  422.5 412.4 %all-reduce.29.cloned.1.call-start = ((), (), s32[]{:S(2)}) async-start(), calls=%async_computation.2 | async-start | bytes 262144 | tf_op jit(solution)/shard_map/psum | solution.py:114
  554.6 9.6 collective-permute-start.9
  562.2 3.1 collective-permute-start.8
  629.4 73.1 %collective-permute-start.10 = (f32[3,128]{1,0:T(4,128)S(1)}, f32[3,128]{1,0:T(4,128)S(1)}, u32[]{:S(2)}, u32[]{:S(2)}) collective-permute-start(f32[3,128]{1,0:T(4,128)S(1)} %get-tuple-element.2083), channel_id=1, source_target_pairs={{0,8},{8,16},{16,24},{24,32},{32,40},{40,48},{48,56},{56,64},{64,7... | collective-permute-start | bytes 4616 | tf_op jit(solution)/shard_map/ppermute | solution.py:26
  665.3 38.1 %collective-permute-start.11 = (f32[3,128]{1,0:T(4,128)S(1)}, f32[3,128]{1,0:T(4,128)S(1)}, u32[]{:S(2)}, u32[]{:S(2)}) collective-permute-start(f32[3,128]{1,0:T(4,128)S(1)} %get-tuple-element.2082), channel_id=1, source_target_pairs={{8,0},{16,8},{24,16},{32,24},{40,32},{48,40},{56,48},{64,56},{72,6... | collective-permute-start | bytes 4616 | tf_op jit(solution)/shard_map/ppermute | solution.py:27
  703.4 0.7 copy-start.10
  704.0 398.5 %all-reduce.31.cloned.1.call-start = ((), (), s32[]{:S(2)}) async-start(), calls=%async_computation.3 | async-start | bytes 262144 | tf_op jit(solution)/shard_map/psum | solution.py:114
  836.0 9.5 collective-permute-start.13
  843.6 3.1 collective-permute-start.12
  895.8 74.3 %collective-permute-start.14 = (f32[3,128]{1,0:T(4,128)S(1)}, f32[3,128]{1,0:T(4,128)S(1)}, u32[]{:S(2)}, u32[]{:S(2)}) collective-permute-start(f32[3,128]{1,0:T(4,128)S(1)} %get-tuple-element.2081), channel_id=1, source_target_pairs={{0,8},{8,16},{16,24},{24,32},{32,40},{40,48},{48,56},{56,64},{64,7... | collective-permute-start | bytes 4616 | tf_op jit(solution)/shard_map/ppermute | solution.py:26
  932.2 170.4 %copy-start.18 = (f32[3,8192]{1,0:T(4,128)S(1)}, f32[3,8192]{1,0:T(4,128)}, u32[]{:S(2)}) copy-start(f32[3,8192]{1,0:T(4,128)} %all-reduce.29.cloned.1.call-done) | copy-start | bytes 294916
  932.2 38.7 %collective-permute-start.15 = (f32[3,128]{1,0:T(4,128)S(1)}, f32[3,128]{1,0:T(4,128)S(1)}, u32[]{:S(2)}, u32[]{:S(2)}) collective-permute-start(f32[3,128]{1,0:T(4,128)S(1)} %get-tuple-element.2080), channel_id=1, source_target_pairs={{8,0},{16,8},{24,16},{32,24},{40,32},{48,40},{56,48},{64,56},{72,6... | collective-permute-start | bytes 4616 | tf_op jit(solution)/shard_map/ppermute | solution.py:27
  971.0 0.7 copy-start.11
  971.6 405.9 %all-reduce.33.cloned.1.call-start = ((), (), s32[]{:S(2)}) async-start(), calls=%async_computation.4 | async-start | bytes 262144 | tf_op jit(solution)/shard_map/psum | solution.py:114
  1103.6 9.6 collective-permute-start.17
  1111.2 3.1 collective-permute-start.16
  1190.4 54.7 %collective-permute-start.18 = (f32[3,128]{1,0:T(4,128)S(1)}, f32[3,128]{1,0:T(4,128)S(1)}, u32[]{:S(2)}, u32[]{:S(2)}) collective-permute-start(f32[3,128]{1,0:T(4,128)S(1)} %get-tuple-element.2079), channel_id=1, source_target_pairs={{0,8},{8,16},{16,24},{24,32},{32,40},{40,48},{48,56},{56,64},{64,7... | collective-permute-start | bytes 4616 | tf_op jit(solution)/shard_map/ppermute | solution.py:26
  1209.5 36.5 %collective-permute-start.19 = (f32[3,128]{1,0:T(4,128)S(1)}, f32[3,128]{1,0:T(4,128)S(1)}, u32[]{:S(2)}, u32[]{:S(2)}) collective-permute-start(f32[3,128]{1,0:T(4,128)S(1)} %get-tuple-element.2078), channel_id=1, source_target_pairs={{8,0},{16,8},{24,16},{32,24},{40,32},{48,40},{56,48},{64,56},{72,6... | collective-permute-start | bytes 4616 | tf_op jit(solution)/shard_map/ppermute | solution.py:27
  1246.0 0.7 copy-start.12
  1246.7 392.1 %all-reduce.35.cloned.1.call-start = ((), (), s32[]{:S(2)}) async-start(), calls=%async_computation.5 | async-start | bytes 262144 | tf_op jit(solution)/shard_map/psum | solution.py:114
  1378.6 9.5 collective-permute-start.21
  1386.2 3.1 collective-permute-start.20
  1435.6 70.9 %collective-permute-start.22 = (f32[3,128]{1,0:T(4,128)S(1)}, f32[3,128]{1,0:T(4,128)S(1)}, u32[]{:S(2)}, u32[]{:S(2)}) collective-permute-start(f32[3,128]{1,0:T(4,128)S(1)} %get-tuple-element.2077), channel_id=1, source_target_pairs={{0,8},{8,16},{16,24},{24,32},{32,40},{40,48},{48,56},{56,64},{64,7... | collective-permute-start | bytes 4616 | tf_op jit(solution)/shard_map/ppermute | solution.py:26
  1470.2 168.5 %copy-start.19 = (f32[3,8192]{1,0:T(4,128)S(1)}, f32[3,8192]{1,0:T(4,128)}, u32[]{:S(2)}) copy-start(f32[3,8192]{1,0:T(4,128)} %all-reduce.33.cloned.1.call-done) | copy-start | bytes 294916
  1470.3 37.0 %collective-permute-start.23 = (f32[3,128]{1,0:T(4,128)S(1)}, f32[3,128]{1,0:T(4,128)S(1)}, u32[]{:S(2)}, u32[]{:S(2)}) collective-permute-start(f32[3,128]{1,0:T(4,128)S(1)} %get-tuple-element.2076), channel_id=1, source_target_pairs={{8,0},{16,8},{24,16},{32,24},{40,32},{48,40},{56,48},{64,56},{72,6... | collective-permute-start | bytes 4616 | tf_op jit(solution)/shard_map/ppermute | solution.py:27
  1507.3 0.7 copy-start.13
  1507.9 405.9 %all-reduce.37.cloned.1.call-start = ((), (), s32[]{:S(2)}) async-start(), calls=%async_computation.6 | async-start | bytes 262144 | tf_op jit(solution)/shard_map/psum | solution.py:114
  1639.8 9.6 collective-permute-start.25
  1647.4 3.1 collective-permute-start.24
  1711.5 70.0 %collective-permute-start.26 = (f32[3,128]{1,0:T(4,128)S(1)}, f32[3,128]{1,0:T(4,128)S(1)}, u32[]{:S(2)}, u32[]{:S(2)}) collective-permute-start(f32[3,128]{1,0:T(4,128)S(1)} %get-tuple-element.2075), channel_id=1, source_target_pairs={{0,8},{8,16},{16,24},{24,32},{32,40},{40,48},{48,56},{56,64},{64,7... | collective-permute-start | bytes 4616 | tf_op jit(solution)/shard_map/ppermute | solution.py:26
  1745.8 36.5 %collective-permute-start.27 = (f32[3,128]{1,0:T(4,128)S(1)}, f32[3,128]{1,0:T(4,128)S(1)}, u32[]{:S(2)}, u32[]{:S(2)}) collective-permute-start(f32[3,128]{1,0:T(4,128)S(1)} %get-tuple-element.2074), channel_id=1, source_target_pairs={{8,0},{16,8},{24,16},{32,24},{40,32},{48,40},{56,48},{64,56},{72,6... | collective-permute-start | bytes 4616 | tf_op jit(solution)/shard_map/ppermute | solution.py:27
  1782.3 0.7 copy-start.14
  1783.0 392.2 %all-reduce.39.cloned.1.call-start = ((), (), s32[]{:S(2)}) async-start(), calls=%async_computation.7 | async-start | bytes 262144 | tf_op jit(solution)/shard_map/psum | solution.py:114
  1914.9 9.8 collective-permute-start.29
  1922.4 3.1 collective-permute-start.28
  1971.8 70.6 %collective-permute-start.30 = (f32[3,128]{1,0:T(4,128)S(1)}, f32[3,128]{1,0:T(4,128)S(1)}, u32[]{:S(2)}, u32[]{:S(2)}) collective-permute-start(f32[3,128]{1,0:T(4,128)S(1)} %get-tuple-element.2073), channel_id=1, source_target_pairs={{0,8},{8,16},{16,24},{24,32},{32,40},{40,48},{48,56},{56,64},{64,7... | collective-permute-start | bytes 4616 | tf_op jit(solution)/shard_map/ppermute | solution.py:26
  2006.3 36.8 %collective-permute-start.31 = (f32[3,128]{1,0:T(4,128)S(1)}, f32[3,128]{1,0:T(4,128)S(1)}, u32[]{:S(2)}, u32[]{:S(2)}) collective-permute-start(f32[3,128]{1,0:T(4,128)S(1)} %get-tuple-element.2072), channel_id=1, source_target_pairs={{8,0},{16,8},{24,16},{32,24},{40,32},{48,40},{56,48},{64,56},{72,6... | collective-permute-start | bytes 4616 | tf_op jit(solution)/shard_map/ppermute | solution.py:27
  2043.1 0.7 copy-start.7
  2043.1 132.1 %copy-start.17 = (f32[3,8192]{1,0:T(4,128)S(1)}, f32[3,8192]{1,0:T(4,128)}, u32[]{:S(2)}) copy-start(f32[3,8192]{1,0:T(4,128)} %all-reduce.37.cloned.1.call-done) | copy-start | bytes 294916
Sparse Core Ops, SparseCore 0:
  154.6 75.6 all-reduce.24
  422.7 79.8 all-reduce.26
  704.2 73.2 all-reduce.28
  971.8 76.6 all-reduce.30
  1246.8 73.4 all-reduce.32
  1508.1 75.6 all-reduce.34
  1783.1 73.1 all-reduce.36
  2043.9 75.9 all-reduce.38
where the time goes:
time: 2200 us; the launch traced here: 2180 us
  blocking collectives  1040 us (47%)
  starting transfers between devices  573 us (26%)
  local copies, waits for them, and re-layouts  384 us (17%)
  other arithmetic  109 us (5%)
  matrix products  44 us (2%)
  between operations  23.1 us (1%)
    psum x8, blocking collectives, on_device(): total = lax.psum(jnp.sum(contact * gap), 'region')  1040 us
    gather x792, local copies, waits for them, and re-layouts  350 us
    ppermute x16, starting transfers between devices, with_halo(): after = lax.ppermute(initial, axis, down)  325 us
    ppermute x16, starting transfers between devices, with_halo(): before = lax.ppermute(last, axis, up)  248 us
  transfers between devices with their start and end apart: 40, of which 15 were waited for; matrix products, arithmetic and copies ran while one was open for 1% of the time, Pallas kernels for 0%

commit v1 on v0

--- a/solution.py
+++ b/solution.py
@@ -1,11 +1,20 @@
+import functools
+
 import jax
 import jax.numpy as jnp
 from jax import lax
+from jax.experimental import pallas as pl
+from jax.experimental.pallas import tpu as pltpu
 from jax.sharding import PartitionSpec as P
 
 NB = 128
 SUBSTEPS = 8
-
+LANES = 8
+OWN = 8
+EXT = 3 * OWN
+ROWS = 256
+EDGE = 24
+AUX = 24
 
 time_step = 0.05
 contact_stiffness = 1.0
@@ -14,6 +23,579 @@
 start_gap = 1.0
 start_speed = 1.0
 group_size = 8
+
+f32, bf16, i32 = jnp.float32, jnp.bfloat16, jnp.int32
+
+
+def iota(shape, dim):
+    return lax.broadcasted_iota(i32, shape, dim)
+
+
+def dot(a, b):
+    return jnp.dot(a, b, preferred_element_type=f32)
+
+
+def dot_t(a, b):
+    return lax.dot_general(a, b, (((1,), (1,)), ((), ())), preferred_element_type=f32)
+
+
+def split2(value):
+    high = value.astype(bf16)
+    return high, (value - high.astype(f32)).astype(bf16)
+
+
+def split3(value):
+    high = value.astype(bf16)
+    rest = value - high.astype(f32)
+    middle = rest.astype(bf16)
+    return high, middle, (rest - middle.astype(f32)).astype(bf16)
+
+
+def take(value, index):
+    return jnp.take_along_axis(value, index, axis=1, mode="promise_in_bounds")
+
+
+def onehot(mask):
+    return jnp.where(mask, 1.0, 0.0).astype(bf16)
+
+
+def cycle_kernel(
+    regions,
+    disp_in, vel_in, mass_in, contact_in, modulus_in, stiff_in, level_in, window_in, conn_in,
+    vel_out, disp_out, react_out,
+    conn_all, aux_all, aux_own, edge_out, edge_in, rim_out, rim_in,
+    first_pay, first_a, first_b, pay, buf_a, pay_b, buf_b,
+    disp, vel, mass, contact, table, slot_cols, kron, tri,
+    wa, wb, back, conn_idx, half, perm, end1, end2, modulus, level, held, state,
+    send_sem, recv_sem, pay_send, first_recv, a_recv, b_recv,
+):
+    r = lax.axis_index("region")
+    lane = lax.axis_index("lane")
+    core = lax.rem(r, 2)
+    chip = r // 2
+    chips = regions // 2
+    up = lax.rem(r + 1, regions)
+    down = lax.rem(r + regions - 1, regions)
+    size_a = 2 * LANES
+    spot_a = lane * 2 + core
+    dt = time_step
+    node_total = regions * LANES * OWN * NB
+    impactor_mass = impactor_ratio * node_total
+
+    def peer_a(k):
+        return (chip * 2 + lax.rem(k, 2), k // 2)
+
+    def peer_b(k):
+        return (k * 2 + core, lane)
+
+    def signal(device):
+        pl.semaphore_signal(
+            pltpu.get_barrier_semaphore(), inc=1, device_id=device,
+            device_id_type=pl.DeviceIdType.MESH,
+        )
+
+    def shifted(spot, step, size):
+        return lax.rem(spot + step, size)
+
+    @pl.loop(1, size_a)
+    def _(k):
+        signal(peer_a(shifted(spot_a, k, size_a)))
+
+    @pl.loop(1, chips)
+    def _(k):
+        signal(peer_b(shifted(chip, k, chips)))
+
+    @pl.when(lane == 0)
+    def _():
+        @pl.loop(0, LANES)
+        def _(j):
+            signal((down, j))
+
+    @pl.when(lane == LANES - 1)
+    def _():
+        @pl.loop(0, LANES)
+        def _(j):
+            signal((up, j))
+
+    def copy(src, dst, send, recv, device):
+        return pltpu.make_async_remote_copy(
+            src_ref=src, dst_ref=dst, send_sem=send, recv_sem=recv,
+            device_id=device, device_id_type=pl.DeviceIdType.MESH,
+        )
+
+    def wait_bytes(ref, sem):
+        pltpu.make_async_copy(ref, ref, sem).wait()
+
+    def load_nodes(place, source_lane):
+        start = pl.multiple_of(source_lane * (OWN * NB), OWN * NB)
+        for j in range(OWN):
+            part = pl.ds(start + j * NB, NB)
+            for c in range(3):
+                disp[c, place + j : place + j + 1, :] = disp_in[c : c + 1, part]
+                vel[c, place + j : place + j + 1, :] = vel_in[c : c + 1, part]
+        rows = pl.ds(pl.multiple_of(source_lane * OWN, OWN), OWN)
+        mass[place : place + OWN, :] = mass_in[rows, :]
+        contact[place : place + OWN, :] = contact_in[rows, :]
+
+    load_nodes(0, jnp.maximum(lane - 1, 0))
+    load_nodes(OWN, lane)
+    load_nodes(2 * OWN, jnp.minimum(lane + 1, LANES - 1))
+
+    rim_lane = jnp.where(lane == 0, LANES - 1, 0)
+    start = pl.multiple_of(rim_lane * (OWN * NB), OWN * NB)
+    for j in range(OWN):
+        part = pl.ds(start + j * NB, NB)
+        for c in range(3):
+            rim_out[8 * c + j : 8 * c + j + 1, :] = disp_in[c : c + 1, part]
+            rim_out[24 + 8 * c + j : 25 + 8 * c + j, :] = vel_in[c : c + 1, part]
+    rows = pl.ds(pl.multiple_of(rim_lane * OWN, OWN), OWN)
+    rim_out[48:56, :] = mass_in[rows, :]
+    rim_out[56:64, :] = contact_in[rows, :]
+
+    own = pl.ds(OWN, OWN)
+    own_contact = contact[own, :]
+    own_mass = mass[own, :]
+    push_rate = (dt * dt * contact_stiffness) * own_contact / own_mass
+    sums = [
+        jnp.sum(own_contact * (start_gap - disp[0, own, :]), axis=0, keepdims=True),
+        jnp.sum(own_contact, axis=0, keepdims=True),
+        jnp.sum(own_contact * push_rate, axis=0, keepdims=True),
+    ]
+    first_pay[...] = jnp.concatenate(sums + [jnp.zeros((5, NB), f32)], axis=0)
+
+    shift = 64 * lax.rem(lane, 2)
+    place = onehot(iota((64, NB), 1) == iota((64, NB), 0) + shift)
+    level_row = level_in[...].astype(f32)
+    window_row = window_in[...].astype(f32)
+    mod_parts = split3(modulus_in[...])
+    mod_rows = sum(
+        lax.dot_general(part, place, (((0,), (0,)), ((), ())), preferred_element_type=f32)
+        for part in mod_parts
+    )
+    pair = jnp.concatenate([level_row, window_row, jnp.zeros((6, 64), f32)], axis=0).astype(bf16)
+    pair_rows = dot(pair, place)
+    aux_own[...] = jnp.concatenate([mod_rows, pair_rows], axis=0)
+
+    before = onehot(iota((64, 64), 0) < iota((64, 64), 1))
+    conn_b = conn_in[...].astype(f32).astype(bf16)
+    low = (window_row <= 7.0).astype(f32)
+    high = (window_row >= 57.0).astype(f32)
+    ends = jnp.concatenate([high, low, jnp.zeros((6, 64), f32)], axis=0)
+    end_rank = dot(ends.astype(bf16), before)
+    end_full = jnp.sum(ends, axis=1, keepdims=True)
+    overflow = jnp.max(jnp.where(end_full > EDGE, 1.0, 0.0), axis=0, keepdims=True)
+    rank_key = jnp.where(ends > 0.0, end_rank, -1.0)
+    mod_wide = [
+        dot(part, onehot(iota((16, NB), 0) == iota((16, NB), 1))).astype(bf16) for part in mod_parts
+    ]
+    for side, offset in ((0, -57.0), (1, 15.0)):
+        pick = onehot(iota((EDGE, 64), 0).astype(f32) == rank_key[side : side + 1, :])
+        edge_out[side, :, :NB] = dot(pick, conn_b)
+        moduli = sum(dot(pick, part) for part in mod_wide)
+        extra = jnp.concatenate(
+            [level_row, window_row + offset, jnp.zeros((6, 64), f32)], axis=0
+        ).astype(bf16)
+        extra_cols = dot_t(pick, extra)
+        spread = onehot(iota((8, NB), 1) == iota((8, NB), 0) + 16)
+        edge_out[side, :, NB:] = moduli + dot(extra_cols.astype(bf16), spread)
+
+    pl.semaphore_wait(pltpu.get_barrier_semaphore(), size_a - 1 + chips - 1 + 2)
+
+    edge_up = copy(edge_out.at[0], edge_in.at[lane], send_sem.at[0], recv_sem.at[0], (up, 0))
+    edge_down = copy(
+        edge_out.at[1], edge_in.at[lane], send_sem.at[1], recv_sem.at[0], (down, LANES - 1)
+    )
+    edge_up.start()
+    edge_down.start()
+    rim_up = copy(rim_out, rim_in, send_sem.at[2], recv_sem.at[1], (up, 0))
+    rim_down = copy(rim_out, rim_in, send_sem.at[2], recv_sem.at[1], (down, LANES - 1))
+
+    @pl.when(lane == 0)
+    def _():
+        rim_up.start()
+
+    @pl.when(lane == LANES - 1)
+    def _():
+        rim_down.start()
+
+    @pl.loop(1, size_a)
+    def _(k):
+        copy(
+            first_pay, first_a.at[spot_a], pay_send.at[0], first_recv.at[0],
+            peer_a(shifted(spot_a, k, size_a)),
+        ).start()
+
+    @pl.loop(1, LANES)
+    def _(k):
+        there = (r, shifted(lane, k, LANES))
+        copy(conn_in, conn_all.at[lane], send_sem.at[3], recv_sem.at[2], there).start()
+        copy(aux_own, aux_all.at[lane], send_sem.at[4], recv_sem.at[3], there).start()
+
+    conn_all[lane] = conn_in[...]
+    aux_all[lane] = aux_own[...]
+    first_a[spot_a] = first_pay[...]
+
+    stiff = split2(stiff_in[...])
+    at = iota((3 * NB, 24), 0)
+    names = onehot((at // NB) * 8 + lax.rem(at, 8) == iota((3 * NB, 24), 1))
+    row_of = lax.rem(iota((3 * NB, 3 * NB), 0), NB) // 8
+    col_of = lax.rem(iota((3 * NB, 3 * NB), 1), NB) // 8
+    same = row_of == col_of
+    for part, places in ((stiff[0], (0, 1)), (stiff[1], (2,))):
+        grown = dot_t(dot_t(names, part).astype(bf16), names)
+        grown = jnp.where(same, grown, 0.0).astype(bf16)
+        for at_place in places:
+            kron[at_place * 3 * NB : (at_place + 1) * 3 * NB, :] = grown
+    running = onehot(iota((NB, NB), 0) <= iota((NB, NB), 1))
+    tri[0:NB, :] = running
+    tri[NB:, :] = running
+
+    @pl.when((lane != 0) & (lane != LANES - 1))
+    def _():
+        edge_in[...] = jnp.zeros_like(edge_in)
+
+    wait_bytes(first_a.at[pl.ds(0, size_a - 1)], first_recv.at[0])
+    total = first_a[0]
+    for k in range(1, size_a):
+        total = total + first_a[k]
+    first_b[chip] = total
+    first_pay2 = first_b.at[chip]
+
+    @pl.loop(1, chips)
+    def _(k):
+        copy(
+            first_pay2, first_b.at[chip], pay_send.at[1], first_recv.at[1],
+            peer_b(shifted(chip, k, chips)),
+        ).start()
+
+    @pl.when((lane == 0) | (lane == LANES - 1))
+    def _():
+        wait_bytes(edge_in, recv_sem.at[0])
+        wait_bytes(rim_in, recv_sem.at[1])
+
+    def unpack_rim(place):
+        for c in range(3):
+            disp[c, place : place + OWN, :] = rim_in[8 * c : 8 * c + 8, :]
+            vel[c, place : place + OWN, :] = rim_in[24 + 8 * c : 32 + 8 * c, :]
+        mass[place : place + OWN, :] = rim_in[48:56, :]
+        contact[place : place + OWN, :] = rim_in[56:64, :]
+
+    @pl.when(lane == 0)
+    def _():
+        unpack_rim(0)
+
+    @pl.when(lane == LANES - 1)
+    def _():
+        unpack_rim(2 * OWN)
+
+    wait_bytes(conn_all.at[pl.ds(0, LANES - 1)], recv_sem.at[2])
+    wait_bytes(aux_all.at[pl.ds(0, LANES - 1)], recv_sem.at[3])
+
+    window_shift = (OWN - 1 - OWN * lane).astype(f32)
+    last_anchor = 2 * OWN + OWN - 2.0
+    columns = []
+    anchors = []
+    for k in range(LANES // 2):
+        aux_pair = aux_all[2 * k] + aux_all[2 * k + 1]
+        anchor = aux_pair[17:18, :] + window_shift
+        padded = jnp.concatenate(
+            [aux_pair[:17, :], anchor, jnp.zeros((NB - 18, NB), f32)], axis=0
+        )
+        columns.append(padded.T)
+        anchors.append(anchor)
+    edge_rows = edge_in[...].reshape(LANES * EDGE, 2 * NB)
+    edge_aux = edge_rows[:, NB:]
+    looked = onehot(iota((8, NB), 1) == iota((8, NB), 0) + 16)
+    edge_look = dot_t(looked, edge_aux.astype(bf16))
+    wanted = [jnp.where((a >= 0.0) & (a <= last_anchor), 1.0, 0.0) for a in anchors]
+    edge_wanted = jnp.where(edge_look[0:1, :] > 0.0, 1.0, 0.0)
+    flags = jnp.concatenate(wanted + [jnp.zeros((4, NB), f32)], axis=0)
+    strict = onehot(iota((NB, NB), 0) < iota((NB, NB), 1))
+    ranks = dot(flags.astype(bf16), strict)
+    edge_count = LANES * EDGE
+    strict_edge = onehot(iota((edge_count, edge_count), 0) < iota((edge_count, edge_count), 1))
+    edge_flags = jnp.concatenate([edge_wanted, jnp.zeros((7, edge_count), f32)], axis=0)
+    edge_ranks = dot(edge_flags.astype(bf16), strict_edge)
+    counts = jnp.sum(flags, axis=1, keepdims=True)
+    picks = []
+    taken = jnp.zeros((1, 1), f32)
+    row_number = iota((ROWS, NB), 0).astype(f32)
+    for k in range(LANES // 2):
+        key = jnp.where(wanted[k] > 0.0, ranks[k : k + 1, :] + taken, -1.0)
+        picks.append(onehot(row_number == key))
+        taken = taken + counts[k : k + 1, :]
+    key = jnp.where(edge_wanted > 0.0, edge_ranks[0:1, :] + taken, -1.0)
+    picks.append(onehot(iota((ROWS, edge_count), 0).astype(f32) == key))
+    taken = taken + jnp.sum(edge_wanted, axis=1, keepdims=True)
+    overflow = jnp.maximum(overflow, jnp.where(taken > float(ROWS), 1.0, 0.0))
+    pick = jnp.concatenate(picks, axis=1)
+    conn_rows = jnp.concatenate(
+        [conn_all[...].astype(f32).reshape(LANES * 64, NB), edge_rows[:, :NB]], axis=0
+    ).astype(bf16)
+    aux_rows = jnp.concatenate(columns + [edge_aux], axis=0)
+    aux_parts = split3(aux_rows)
+    conn = dot(pick, conn_rows)
+    aux = dot(pick, aux_parts[0]) + dot(pick, aux_parts[1]) + dot(pick, aux_parts[2])
+
+    lane_no = iota((ROWS, NB), 1)
+    modulus[...] = take(aux, lane_no // 8)
+    level[...] = take(aux, jnp.full((ROWS, NB), 16, i32)).astype(i32) - 1
+    anchor = take(aux, jnp.full((ROWS, NB), 17, i32)).astype(i32)
+    wa[...] = onehot((lane_no & 31) == anchor)
+    wb[...] = onehot((lane_no & 31) == anchor + 1)
+    anchor_row = aux.T[17:18, :].astype(i32)
+    ext_row = iota((32, ROWS), 0)
+    back_a = onehot(ext_row == anchor_row)
+    back_b = onehot(ext_row == anchor_row + 1)
+    back[...] = jnp.concatenate([back_a, back_b, back_a, back_b], axis=1)
+    conn_i = conn.astype(i32)
+    conn_idx[...] = conn_i & (NB - 1)
+    half[...] = conn_i >> 7
+
+    keys = conn * float(NB) + lane_no.astype(f32)
+    span = 2
+    while span <= NB:
+        step = span // 2
+        while step >= 1:
+            other = take(keys, lane_no ^ step)
+            keep_low = ((lane_no & step) == 0) == ((lane_no & span) == 0)
+            keys = jnp.where(keep_low, jnp.minimum(keys, other), jnp.maximum(keys, other))
+            step //= 2
+        span *= 2
+    keys_i = keys.astype(i32)
+    perm[...] = keys_i & (NB - 1)
+    nodes = keys_i >> 7
+    for ref, base in ((end1, 0), (end2, NB)):
+        target = lane_no + base
+        found = jnp.zeros((ROWS, NB), i32)
+        for step in (64, 32, 16, 8, 4, 2, 1, 0):
+            probe = take(nodes, found + (step - 1 if step else 0))
+            found = jnp.where(probe <= target, found + max(step, 1), found)
+        ref[...] = found - 1
+
+    held[...] = jnp.zeros_like(held)
+    table[...] = jnp.zeros_like(table)
+
+    wait_bytes(first_b.at[pl.ds(0, chips - 1)], first_recv.at[1])
+    total = first_b[0]
+    for k in range(1, chips):
+        total = total + first_b[k]
+    first = jnp.sum(total, axis=1, keepdims=True)
+    reaction0, contact_sum, push_sum = first[0:1, :], first[1:2, :], first[2:3, :]
+    zero_row = jnp.zeros((1, NB), f32)
+    gap1 = jnp.full((1, NB), start_gap, f32)
+    w1 = start_speed - dt * contact_stiffness * (reaction0 + zero_row) / impactor_mass
+    state[0:1, :] = gap1
+    state[1:2, :] = gap1 + dt * w1
+    state[2:3, :] = w1
+    state[3:4, :] = contact_sum + zero_row
+    state[4:5, :] = push_sum + zero_row
+    react_out[0:1, :] = (reaction0 + zero_row) / node_total
+    poison = jnp.where(overflow > 0.0, jnp.inf, 0.0) + zero_row
+    state[5:6, :] = poison
+
+    first_lane = iota((ROWS, NB), 1) == 0
+
+    def forces(s):
+        parts = [split3(disp[c]) for c in range(3)]
+        for k in range(3):
+            table[32 * k : 32 * k + EXT, :] = jnp.concatenate([parts[c][k] for c in range(3)], axis=1)
+        source = table[...]
+        near = dot(wa[...], source)
+        far = dot(wb[...], source)
+        index = conn_idx[...]
+        second = half[...] > 0
+        slots = []
+        for c in range(3):
+            cols = slice(c * NB, (c + 1) * NB)
+            slots.append(jnp.where(second, take(far[:, cols], index), take(near[:, cols], index)))
+        spread = jnp.concatenate(slots, axis=1)
+        top, rest = split2(spread)
+        strain = dot(jnp.concatenate([top, rest, top], axis=1), kron[...])
+        active = (level[...] & s) == 0
+        order = perm[...]
+        mod = modulus[...]
+        e1 = end1[...]
+        e2 = end2[...]
+        for c in range(3):
+            g = strain[:, c * NB : (c + 1) * NB]
+            fresh = mod * (g + hardening * g * g * g)
+            now = jnp.where(active, fresh, held[c])
+            held[c] = now
+            sorted_force = take(now, order)
+            sums = dot(jnp.concatenate(split2(sorted_force), axis=1), tri[...])
+            upto1 = jnp.where(e1 >= 0, take(sums, e1 & (NB - 1)), 0.0)
+            upto2 = jnp.where(e2 >= 0, take(sums, e2 & (NB - 1)), 0.0)
+            prev1 = pltpu.roll(upto1, 1, 1)
+            prev2 = pltpu.roll(upto2, 1, 1)
+            f1 = split2(upto1 - jnp.where(first_lane, 0.0, prev1))
+            f2 = split2(upto2 - jnp.where(first_lane, prev1, prev2))
+            cols = slice(c * NB, (c + 1) * NB)
+            slot_cols[0:ROWS, cols] = f1[0]
+            slot_cols[ROWS : 2 * ROWS, cols] = f2[0]
+            slot_cols[2 * ROWS : 3 * ROWS, cols] = f1[1]
+            slot_cols[3 * ROWS :, cols] = f2[1]
+        return dot(back[...], slot_cols[...])
+
+    def relay(s):
+        wait_bytes(buf_a.at[s, pl.ds(0, size_a - 1)], a_recv.at[s])
+        value = buf_a[s, 0]
+        for k in range(1, size_a):
+            value = value + buf_a[s, k]
+        buf_b[s, chip] = value
+
+        @pl.loop(1, chips)
+        def _(k):
+            copy(
+                buf_b.at[s, chip], buf_b.at[s, chip], pay_send.at[3], b_recv.at[s],
+                peer_b(shifted(chip, k, chips)),
+            ).start()
+
+    def collect(s):
+        wait_bytes(buf_b.at[s, pl.ds(0, chips - 1)], b_recv.at[s])
+        value = buf_b[s, 0]
+        for k in range(1, chips):
+            value = value + buf_b[s, k]
+        total = jnp.sum(value, axis=1, keepdims=True) + zero_row
+        before_z = state[0:1, :]
+        now_z = state[1:2, :]
+        reaction = total + (now_z - start_gap) * state[3:4, :] - before_z * state[4:5, :]
+        react_out[pl.ds(s + 1, 1), :] = reaction / node_total
+        speed = state[2:3, :] - dt * contact_stiffness * reaction / impactor_mass
+        state[0:1, :] = now_z
+        state[1:2, :] = now_z + dt * speed
+        state[2:3, :] = speed
+
+    def substep(s, z_row_of):
+        force = forces(s)
+        ext_no = iota((EXT, NB), 0)
+        valid = (ext_no >= 1 + s) & (ext_no <= EXT - 2 - s)
+        weight = contact[...]
+        inverse = 1.0 / mass[...]
+        based = []
+        for c in range(3):
+            pull = -force[:EXT, c * NB : (c + 1) * NB]
+            if c == 0:
+                pull = pull - contact_stiffness * weight * disp[0]
+            based.append(vel[c] + dt * (pull * inverse))
+        free = disp[0, own, :] + dt * based[0][OWN : 2 * OWN]
+        part = jnp.sum(contact[own, :] * (start_gap - free), axis=0, keepdims=True)
+        pay[s] = part + state[5:6, :]
+        buf_a[s, spot_a] = pay[s]
+
+        @pl.when(s < SUBSTEPS - 1)
+        def _():
+            @pl.loop(1, size_a)
+            def _(k):
+                copy(
+                    pay.at[s], buf_a.at[s, spot_a], pay_send.at[2], a_recv.at[s],
+                    peer_a(shifted(spot_a, k, size_a)),
+                ).start()
+
+        @pl.when((s == 2) | (s == 5))
+        def _():
+            @pl.loop(0, 3)
+            def _(k):
+                relay(s - 2 + k)
+
+        @pl.when(s >= 2)
+        def _():
+            collect(s - 2)
+
+        z_now = z_row_of(s)
+        based[0] = based[0] + (dt * contact_stiffness) * z_now * (weight * inverse)
+        for c in range(3):
+            vel[c] = jnp.where(valid, based[c], vel[c])
+            disp[c] = jnp.where(valid, disp[c] + dt * based[c], disp[c])
+
+    def z_row_of(s):
+        return jnp.where(s == 0, start_gap, state[1:2, :])
+
+    def gather_out(ref, slot):
+        @pl.loop(1, LANES)
+        def _(k):
+            there = (r, shifted(lane, k, LANES))
+            copy(
+                ref.at[lane], ref.at[lane], send_sem.at[5 + slot], recv_sem.at[4 + slot], there
+            ).start()
+
+    @pl.loop(0, SUBSTEPS)
+    def _(s):
+        substep(s, z_row_of)
+
+        @pl.when(s == SUBSTEPS - 2)
+        def _():
+            for c in range(3):
+                disp_out[lane, c] = disp[c, own, :]
+            gather_out(disp_out, 0)
+
+    for c in range(3):
+        vel_out[lane, c] = vel[c, own, :]
+    gather_out(vel_out, 1)
+    relay(SUBSTEPS - 2)
+    collect(SUBSTEPS - 2)
+    wait_bytes(disp_out.at[pl.ds(0, LANES - 1)], recv_sem.at[4])
+    wait_bytes(vel_out.at[pl.ds(0, LANES - 1)], recv_sem.at[5])
+
+    edge_up.wait_send()
+    edge_down.wait_send()
+
+    @pl.when((lane == 0) | (lane == LANES - 1))
+    def _():
+        rim_up.wait_send()
+
+    wait_bytes(conn_all.at[pl.ds(0, LANES - 1)], send_sem.at[3])
+    wait_bytes(aux_all.at[pl.ds(0, LANES - 1)], send_sem.at[4])
+    wait_bytes(disp_out.at[pl.ds(0, LANES - 1)], send_sem.at[5])
+    wait_bytes(vel_out.at[pl.ds(0, LANES - 1)], send_sem.at[6])
+    wait_bytes(first_a.at[pl.ds(0, size_a - 1)], pay_send.at[0])
+    wait_bytes(first_b.at[pl.ds(0, chips - 1)], pay_send.at[1])
+    wait_bytes(buf_a.at[pl.ds(0, SUBSTEPS - 1), pl.ds(0, size_a - 1)], pay_send.at[2])
+    wait_bytes(buf_b.at[pl.ds(0, SUBSTEPS - 1), pl.ds(0, chips - 1)], pay_send.at[3])
+
+
+def run_cycle(regions, init_disp, init_vel, mass, contact, modulus, stiffness, levels, windows, conn):
+    chips = regions // 2
+    vmem = pl.BlockSpec(memory_space=pltpu.VMEM)
+    V = pltpu.VMEM
+    vel, disp, react = pl.pallas_call(
+        functools.partial(cycle_kernel, regions),
+        out_shape=(
+            jax.ShapeDtypeStruct((LANES, 3, OWN, NB), f32),
+            jax.ShapeDtypeStruct((LANES, 3, OWN, NB), f32),
+            jax.ShapeDtypeStruct((SUBSTEPS, NB), f32),
+        ),
+        in_specs=[vmem] * 9,
+        out_specs=[vmem] * 3,
+        scratch_shapes=[
+            V((LANES, 64, NB), i32), V((LANES, AUX, NB), f32), V((AUX, NB), f32),
+            V((2, EDGE, 2 * NB), f32), V((LANES, EDGE, 2 * NB), f32),
+            V((64, NB), f32), V((64, NB), f32),
+            V((8, NB), f32), V((2 * LANES, 8, NB), f32), V((chips, 8, NB), f32),
+            V((SUBSTEPS, 1, NB), f32), V((SUBSTEPS, 2 * LANES, 1, NB), f32),
+            V((SUBSTEPS, 1, NB), f32), V((SUBSTEPS, chips, 1, NB), f32),
+            V((3, EXT, NB), f32), V((3, EXT, NB), f32), V((EXT, NB), f32), V((EXT, NB), f32),
+            V((NB, 3 * NB), bf16), V((4 * ROWS, 3 * NB), bf16),
+            V((9 * NB, 3 * NB), bf16), V((2 * NB, NB), bf16),
+            V((ROWS, NB), bf16), V((ROWS, NB), bf16), V((32, 4 * ROWS), bf16),
+            V((ROWS, NB), i32), V((ROWS, NB), i32), V((ROWS, NB), i32),
+            V((ROWS, NB), i32), V((ROWS, NB), i32),
+            V((ROWS, NB), f32), V((ROWS, NB), i32), V((3, ROWS, NB), f32), V((8, NB), f32),
+            pltpu.SemaphoreType.DMA((7,)), pltpu.SemaphoreType.DMA((6,)),
+            pltpu.SemaphoreType.DMA((4,)), pltpu.SemaphoreType.DMA((2,)),
+            pltpu.SemaphoreType.DMA((SUBSTEPS,)), pltpu.SemaphoreType.DMA((SUBSTEPS,)),
+        ],
+        compiler_params=pltpu.CompilerParams(
+            collective_id=0, has_side_effects=True, vmem_limit_bytes=48 * 1024 * 1024
+        ),
+        name="crush_cycle",
+    )(
+        init_disp, init_vel, mass.reshape(-1, NB), contact.reshape(-1, NB), modulus, stiffness,
+        levels.reshape(1, -1), windows.reshape(1, -1), conn,
+    )
+    velocity = vel.transpose(1, 0, 2, 3).reshape(3, -1)
+    displacement = disp.transpose(1, 0, 2, 3).reshape(3, -1) + time_step * velocity
+    return displacement, velocity, react[:, 0]
 
 
 def with_halo(array, sides, width):
@@ -42,7 +624,7 @@
     )
 
 
-def on_device(init_disp, init_vel, mass, contact, modulus, stiffness, levels, windows, conn):
+def plain_cycle(init_disp, init_vel, mass, contact, modulus, stiffness, levels, windows, conn):
     region_count = lax.axis_size("region")
     node_region = init_disp.shape[1]
     slot_count = conn.shape[1]
@@ -126,6 +708,13 @@
     return (disp_full, vel_state, jnp.stack(history))
 
 
+def on_device(*arguments):
+    regions = lax.axis_size("region")
+    fast = run_cycle(regions, *arguments)
+    fits = jnp.all(jnp.isfinite(fast[2]))
+    return lax.cond(fits, lambda: fast, lambda: plain_cycle(*arguments))
+
+
 def solution(mesh):
     in_specs = (
         P(None, "region"),

time: 2200 us -> 94.7 us (0.04)
  blocking collectives: 1040 us -> 0 us
  starting transfers between devices: 573 us -> 0 us
  local copies, waits for them, and re-layouts: 384 us -> 1.6 us
  other arithmetic: 109 us -> 1.49 us
  Pallas kernels: 0 us -> 76.3 us
  matrix products: 44 us -> 0 us
    psum x8 -> x0, blocking collectives: 1040 us -> none  [on_device(): total = lax.psum(jnp.sum(contact * gap), 'region')]
    ppermute x32 -> x0, starting transfers between devices: 573 us -> none  [the longest x16 325 us: with_halo(): after = lax.ppermute(initial, axis, down)]
    gather x796 -> x0, local copies, waits for them, and re-layouts: 352 us -> none
    pallas_call x0 -> x1, Pallas kernels: none -> 76.3 us  [run_cycle(): pl.pallas_call(functools.partial(cycle_kernel, regions), out_shape=(jax.S...]
    scatter-add x82 -> x0, other arithmetic: 61 us -> none  [the longest x33 27.8 us: one_group(): totals.at[level_group, :, window_group + 1].add(window_force[:, :, 1])]
    dot_general x99 -> x0, matrix products: 44 us -> none  [the longest x33 18.6 us: one_group(): jnp.einsum('gcs,gws->gcw', slot_force, onehot, precision=lax.Precision.HI...]
  transfers between devices with their start and end apart: 40 -> 0, of which waited for: 15 -> 0; matrix products, arithmetic and copies ran while one was open for 1% -> 0% of each run, Pallas kernels for 0% -> 0%
where the time goes in v1:
time: 94.7 us; the launch traced here: 94.4 us
  Pallas kernels  76.3 us (81%)
  between operations  14.8 us (16%)
  local copies, waits for them, and re-layouts  1.6 us (2%)
  other arithmetic  1.49 us (2%)
    pallas_call x1, Pallas kernels, run_cycle(): pl.pallas_call(functools.partial(cycle_kernel, regions), out_shape=(jax.S...  76.3 us

profile of v1, /device:TPU:1, one launch (start us, length us, event | category | flops | bytes accessed | tf_op | source)
XLA Modules:
  0.0 94.4 jit_solution(7137795336011766398)
XLA Ops:
  7.2 0.0 copy-start.3
  7.2 0.0 copy-start.2
  7.2 0.8 copy.278.modulus_in
  8.0 0.0 copy-start
  8.0 0.0 copy-start.1
  8.0 0.0 copy-done.3
  8.0 0.0 copy-done.2
  8.0 0.6 copy-done
  8.6 0.0 copy-done.1
  8.6 0.0 copy-start.4
  8.7 0.0 copy-start.5
  8.7 0.0 copy-start.6
  8.7 0.0 copy-start.7
  8.7 76.3 %crush_cycle.1 = (f32[8,3,8,128]{3,2,1,0:T(8,128)S(1)}, f32[8,3,8,128]{3,2,1,0:T(8,128)S(1)}, f32[8,128]{1,0:T(8,128)S(1)}) custom-call(f32[3,8192]{1,0:T(4,128)} %disp_in.1, f32[3,8192]{1,0:T(4,128)} %vel_in.1, f32[64,128]{1,0:T(8,128)S(1)} %bitcast.675, f32[64,128]{1,0:T(8,128)} %bitcast.676, f32[64,16]{1,0:T(8,128)S(1)} %copy.278.modulus_in, ...), custom_call_target="tpu_custom_call" | custom-call | tf_op jit(solution)/shard_map/crush_cycle/pallas_call | solution.py:561
  85.0 0.0 copy-start.20
  85.0 0.1 slice_reduce_fusion
  85.1 0.0 copy-start.21
  85.1 0.6 is-finite_reduce_fusion
  85.8 0.0 copy-done.21
  86.4 0.0 copy-done.4
  86.4 0.0 copy-done.5
  86.5 0.0 copy-done.6
  86.5 0.0 copy-done.7
  86.5 0.0 copy-done.20
  86.5 1.1 %conditional.1 = (f32[3,8192]{1,0:T(4,128)}, f32[3,8192]{1,0:T(4,128)}, f32[8]{0:T(128)}) conditional(s32[]{:T(128)} %convert_element_type.22, (f32[3,8192]{1,0:T(4,128)S(1)}, f32[8192]{0:T(1024)S(1)}, s32[64]{0:T(128)S(1)}, s32[64,128]{1,0:T(8,128)S(1)}, s32[64]{0:T(128)S(1)}, /*index=5*/f32[64,16]{0,1:T(8,128)S(1)}, f32[24,24]{1,0:T(8,128)S(1)}, ...), branch_computations={%region_1.72_spmd, %region_72.73_spmd} | conditional | flops 165457744 | bytes 30049216 | solution.py:715
  86.8 0.9 bitcast_add_fusion
  (1 shorter events, 0.0 us)
Async XLA Ops:
  7.2 0.8 copy-start.3
  7.2 0.8 copy-start.2
  8.0 0.7 copy-start
  8.0 0.7 copy-start.1
  8.6 77.8 %copy-start.4 = (f32[8192]{0:T(1024)S(1)}, f32[8192]{0:T(1024)}, u32[]{:S(2)}) copy-start(f32[8192]{0:T(1024)} %param.99) | copy-start | bytes 98308
  8.7 77.8 %copy-start.5 = (s32[64,128]{1,0:T(8,128)S(1)}, s32[64,128]{1,0:T(8,128)}, u32[]{:S(2)}) copy-start(s32[64,128]{1,0:T(8,128)} %conn_in.1) | copy-start | bytes 98308
  8.7 77.8 %copy-start.6 = (f32[3,8192]{1,0:T(4,128)S(1)}, f32[3,8192]{1,0:T(4,128)}, u32[]{:S(2)}) copy-start(f32[3,8192]{1,0:T(4,128)} %disp_in.1) | copy-start | bytes 294916
  8.7 77.8 %copy-start.7 = (f32[3,8192]{1,0:T(4,128)S(1)}, f32[3,8192]{1,0:T(4,128)}, u32[]{:S(2)}) copy-start(f32[3,8192]{1,0:T(4,128)} %vel_in.1) | copy-start | bytes 294916
  85.0 1.5 %copy-start.20 = (f32[64,16]{0,1:T(8,128)S(1)}, f32[64,16]{0,1:T(8,128)}, u32[]{:S(2)}) copy-start(f32[64,16]{0,1:T(8,128)} %param.100) | copy-start | bytes 12292
  85.1 0.6 copy-start.21

commit v2 on v1

--- a/solution.py
+++ b/solution.py
@@ -61,13 +61,14 @@
 
 def cycle_kernel(
     regions,
+    disp_far, vel_far, mass_far, contact_far, modulus_far, stiff_far, level_far, window_far, conn_far,
+    vel_out, disp_out, react_out, flag_out,
     disp_in, vel_in, mass_in, contact_in, modulus_in, stiff_in, level_in, window_in, conn_in,
-    vel_out, disp_out, react_out,
     conn_all, aux_all, aux_own, edge_out, edge_in, rim_out, rim_in,
     first_pay, first_a, first_b, pay, buf_a, pay_b, buf_b,
     disp, vel, mass, contact, table, slot_cols, kron, tri,
     wa, wb, back, conn_idx, half, perm, end1, end2, modulus, level, held, state,
-    send_sem, recv_sem, pay_send, first_recv, a_recv, b_recv,
+    send_sem, recv_sem, pay_send, first_recv, a_recv, b_recv, load_sem,
 ):
     r = lax.axis_index("region")
     lane = lax.axis_index("lane")
@@ -126,6 +127,17 @@
     def wait_bytes(ref, sem):
         pltpu.make_async_copy(ref, ref, sem).wait()
 
+    loads = []
+    for k, (far, here) in enumerate((
+        (level_far, level_in), (window_far, window_in), (modulus_far, modulus_in),
+        (conn_far, conn_in), (contact_far, contact_in), (mass_far, mass_in),
+        (disp_far, disp_in), (vel_far, vel_in), (stiff_far, stiff_in),
+    )):
+        loads.append(pltpu.make_async_copy(far, here, load_sem.at[k]))
+        loads[-1].start()
+    for load in loads:
+        load.wait()
+
     def load_nodes(place, source_lane):
         start = pl.multiple_of(source_lane * (OWN * NB), OWN * NB)
         for j in range(OWN):
@@ -169,8 +181,7 @@
     window_row = window_in[...].astype(f32)
     mod_parts = split3(modulus_in[...])
     mod_rows = sum(
-        lax.dot_general(part, place, (((0,), (0,)), ((), ())), preferred_element_type=f32)
-        for part in mod_parts
+        dot(part, place) for part in mod_parts
     )
     pair = jnp.concatenate([level_row, window_row, jnp.zeros((6, 64), f32)], axis=0).astype(bf16)
     pair_rows = dot(pair, place)
@@ -185,13 +196,13 @@
     end_full = jnp.sum(ends, axis=1, keepdims=True)
     overflow = jnp.max(jnp.where(end_full > EDGE, 1.0, 0.0), axis=0, keepdims=True)
     rank_key = jnp.where(ends > 0.0, end_rank, -1.0)
-    mod_wide = [
-        dot(part, onehot(iota((16, NB), 0) == iota((16, NB), 1))).astype(bf16) for part in mod_parts
-    ]
     for side, offset in ((0, -57.0), (1, 15.0)):
         pick = onehot(iota((EDGE, 64), 0).astype(f32) == rank_key[side : side + 1, :])
         edge_out[side, :, :NB] = dot(pick, conn_b)
-        moduli = sum(dot(pick, part) for part in mod_wide)
+        moduli = sum(
+            dot(dot_t(pick, part).astype(bf16), onehot(iota((16, NB), 0) == iota((16, NB), 1)))
+            for part in mod_parts
+        )
         extra = jnp.concatenate(
             [level_row, window_row + offset, jnp.zeros((6, 64), f32)], axis=0
         ).astype(bf16)
@@ -537,6 +548,9 @@
     wait_bytes(disp_out.at[pl.ds(0, LANES - 1)], recv_sem.at[4])
     wait_bytes(vel_out.at[pl.ds(0, LANES - 1)], recv_sem.at[5])
 
+    whole = jnp.where(jnp.abs(react_out[...]) < jnp.inf, 0, 1)
+    flag_out[0] = jnp.max(whole)
+
     edge_up.wait_send()
     edge_down.wait_send()
 
@@ -558,16 +572,20 @@
     chips = regions // 2
     vmem = pl.BlockSpec(memory_space=pltpu.VMEM)
     V = pltpu.VMEM
-    vel, disp, react = pl.pallas_call(
+    vel, disp, react, flag = pl.pallas_call(
         functools.partial(cycle_kernel, regions),
         out_shape=(
             jax.ShapeDtypeStruct((LANES, 3, OWN, NB), f32),
             jax.ShapeDtypeStruct((LANES, 3, OWN, NB), f32),
             jax.ShapeDtypeStruct((SUBSTEPS, NB), f32),
+            jax.ShapeDtypeStruct((1,), i32),
         ),
-        in_specs=[vmem] * 9,
-        out_specs=[vmem] * 3,
+        in_specs=[pl.BlockSpec(memory_space=pl.ANY)] * 9,
+        out_specs=[vmem] * 3 + [pl.BlockSpec(memory_space=pltpu.SMEM)],
         scratch_shapes=[
+            V(init_disp.shape, f32), V(init_vel.shape, f32), V((LANES * OWN, NB), f32),
+            V((LANES * OWN, NB), f32), V((16, 64), f32), V((24, 24), f32),
+            V((1, 64), i32), V((1, 64), i32), V((64, NB), i32),
             V((LANES, 64, NB), i32), V((LANES, AUX, NB), f32), V((AUX, NB), f32),
             V((2, EDGE, 2 * NB), f32), V((LANES, EDGE, 2 * NB), f32),
             V((64, NB), f32), V((64, NB), f32),
@@ -584,18 +602,28 @@
             pltpu.SemaphoreType.DMA((7,)), pltpu.SemaphoreType.DMA((6,)),
             pltpu.SemaphoreType.DMA((4,)), pltpu.SemaphoreType.DMA((2,)),
             pltpu.SemaphoreType.DMA((SUBSTEPS,)), pltpu.SemaphoreType.DMA((SUBSTEPS,)),
+            pltpu.SemaphoreType.DMA((9,)),
         ],
         compiler_params=pltpu.CompilerParams(
             collective_id=0, has_side_effects=True, vmem_limit_bytes=48 * 1024 * 1024
         ),
         name="crush_cycle",
     )(
-        init_disp, init_vel, mass.reshape(-1, NB), contact.reshape(-1, NB), modulus, stiffness,
+        init_disp, init_vel, mass.reshape(-1, NB), contact.reshape(-1, NB), modulus.T, stiffness,
         levels.reshape(1, -1), windows.reshape(1, -1), conn,
     )
     velocity = vel.transpose(1, 0, 2, 3).reshape(3, -1)
     displacement = disp.transpose(1, 0, 2, 3).reshape(3, -1) + time_step * velocity
-    return displacement, velocity, react[:, 0]
+    return (displacement, velocity, react[:, 0]), flag[0]
+
+
+def sum_over(value, axis):
+    count = lax.axis_size(axis)
+    step = 1
+    while step < count:
+        value = value + lax.ppermute(value, axis, [(i, i ^ step) for i in range(count)])
+        step *= 2
+    return value
 
 
 def with_halo(array, sides, width):
@@ -693,10 +721,10 @@
         partial_force = force_ext[:, block_rows:-block_rows]
         partial_force = partial_force.at[:, :block_rows].add(rim_terms[:, :block_rows])
         partial_force = partial_force.at[:, -block_rows:].add(rim_terms[:, -block_rows:])
-        force = lax.psum(partial_force, "lane")
+        force = sum_over(partial_force, "lane")
         disp_state = disp_full
         gap = gap_now - disp_state[0]
-        total = lax.psum(jnp.sum(contact * gap), "region")
+        total = sum_over(jnp.sum(contact * gap), "region")
         history.append(total / node_total)
         push = jnp.zeros_like(force).at[0].set(contact_stiffness * contact * gap)
         accel = (push - force) / mass[None, :]
@@ -710,9 +738,8 @@
 
 def on_device(*arguments):
     regions = lax.axis_size("region")
-    fast = run_cycle(regions, *arguments)
-    fits = jnp.all(jnp.isfinite(fast[2]))
-    return lax.cond(fits, lambda: fast, lambda: plain_cycle(*arguments))
+    fast, flag = run_cycle(regions, *arguments)
+    return lax.cond(flag == 0, lambda: fast, lambda: plain_cycle(*arguments))
 
 
 def solution(mesh):

time: 94.7 us -> 80.6 us (0.85)
  between operations: 14.8 us -> 1.32 us
where the time goes in v2:
time: 80.6 us; the launch traced here: 80.3 us
  Pallas kernels  76.5 us (95%)
  local copies, waits for them, and re-layouts  1.4 us (2%)
  between operations  1.32 us (2%)
  other arithmetic  0.85 us (1%)
    pallas_call x1, Pallas kernels, run_cycle(): pl.pallas_call(functools.partial(cycle_kernel, regions), out_shape=(jax.S...  76.5 us

profile of v2, /device:TPU:1, one launch (start us, length us, event | category | flops | bytes accessed | tf_op | source)
XLA Modules:
  0.0 80.3 jit_solution(6786764202754833196)
XLA Ops:
  0.6 0.0 copy-start.8
  0.6 0.0 copy-start
  0.7 0.0 copy-start.1
  0.7 0.7 copy-done.8
  1.3 0.0 copy-done
  1.3 0.0 copy-done.1
  1.3 0.0 copy-start.3
  1.3 0.0 copy-start.4
  1.3 0.0 copy-start.5
  1.4 0.0 copy-start.6
  1.4 0.0 copy-start.7
  1.4 76.5 %crush_cycle.1 = (f32[8,3,8,128]{3,2,1,0:T(8,128)S(1)}, f32[8,3,8,128]{3,2,1,0:T(8,128)S(1)}, f32[8,128]{1,0:T(8,128)S(1)}, s32[1]{0:T(128)}) custom-call(f32[3,8192]{1,0:T(4,128)} %disp_far.1, f32[3,8192]{1,0:T(4,128)} %vel_far.1, f32[64,128]{1,0:T(8,128)} %bitcast.680, f32[64,128]{1,0:T(8,128)} %bitcast.679, f32[16,64]{1,0:T(8,128)S(1)} %bitcast.739, ...), custom_call_target="tpu_custom_call" | custom-call | tf_op jit(solution)/shard_map/crush_cycle/pallas_call | solution.py:575
  77.9 0.0 copy-start.2
  78.5 0.0 copy-done.3
  78.5 0.0 copy-done.4
  78.5 0.0 copy-done.5
  78.5 0.0 copy-done.6
  78.5 0.0 copy-done.7
  78.5 0.1 copy-done.2
  78.6 1.7 %conditional.1 = (f32[3,8192]{1,0:T(4,128)}, f32[3,8192]{1,0:T(4,128)}, f32[8]{0:T(128)}) conditional(s32[]{:T(128)} %bitcast.38, (f32[3,8192]{1,0:T(4,128)S(1)}, f32[8192]{0:T(1024)S(1)}, s32[64]{0:T(128)S(1)}, s32[64,128]{1,0:T(8,128)S(1)}, s32[64]{0:T(128)S(1)}, /*index=5*/f32[64,16]{0,1:T(8,128)S(1)}, f32[24,24]{1,0:T(8,128)S(1)}, ...), branch_computations={%region_0.55_spmd, %region_55.56_spmd} | conditional | flops 165457744 | bytes 34902380 | solution.py:742
  78.8 0.9 %bitcast_add_fusion = (f32[3,8192]{1,0:T(4,128)}, f32[3,8192]{1,0:T(4,128)}) fusion(f32[1,3,64,128]{3,2,1,0:T(8,128)S(1)} %get-tuple-element.2181, f32[1,3,64,128]{3,2,1,0:T(8,128)S(1)} %get-tuple-element.2180), kind=kLoop, calls=%fused_computation.29 | loop fusion | flops 49152 | bytes 393216 | tf_op jit(solution)/shard_map/add | solution.py:616
  79.7 0.1 copy.281
  79.8 0.5 slice_bitcast_fusion
  (1 shorter events, 0.0 us)
Async XLA Ops:
  0.6 0.7 copy-start.8
  0.6 0.7 copy-start
  0.7 0.7 copy-start.1
  1.3 77.1 %copy-start.3 = (f32[8192]{0:T(1024)S(1)}, f32[8192]{0:T(1024)}, u32[]{:S(2)}) copy-start(f32[8192]{0:T(1024)} %param.99) | copy-start | bytes 98308
  1.3 77.2 %copy-start.4 = (s32[64,128]{1,0:T(8,128)S(1)}, s32[64,128]{1,0:T(8,128)}, u32[]{:S(2)}) copy-start(s32[64,128]{1,0:T(8,128)} %conn_far.1) | copy-start | bytes 98308
  1.3 77.2 %copy-start.5 = (f32[8192]{0:T(1024)S(1)}, f32[8192]{0:T(1024)}, u32[]{:S(2)}) copy-start(f32[8192]{0:T(1024)} %param.98) | copy-start | bytes 98308
  1.4 77.2 %copy-start.6 = (f32[3,8192]{1,0:T(4,128)S(1)}, f32[3,8192]{1,0:T(4,128)}, u32[]{:S(2)}) copy-start(f32[3,8192]{1,0:T(4,128)} %disp_far.1) | copy-start | bytes 294916
  1.4 77.2 %copy-start.7 = (f32[3,8192]{1,0:T(4,128)S(1)}, f32[3,8192]{1,0:T(4,128)}, u32[]{:S(2)}) copy-start(f32[3,8192]{1,0:T(4,128)} %vel_far.1) | copy-start | bytes 294916
  77.9 0.7 copy-start.2

commit v3 on v2

v3 whole, which is shorter than its diff:
```python
import functools

import jax
import jax.numpy as jnp
from jax import lax
from jax.experimental import pallas as pl
from jax.experimental.pallas import tpu as pltpu
from jax.sharding import PartitionSpec as P

NB = 128
SUBSTEPS = 8
LANES = 8
OWN = 8
DEPTH = 3
NODE_ROWS = 16
ANCHORS = OWN - 1 + 2 * DEPTH
ROWS = 160
PACK = 32
EDGE = 16

time_step = 0.05
contact_stiffness = 1.0
hardening = 2.0
impactor_ratio = 0.05
start_gap = 1.0
start_speed = 1.0
group_size = 8

f32, bf16, i32 = jnp.float32, jnp.bfloat16, jnp.int32


def iota(shape, dim):
    return lax.broadcasted_iota(i32, shape, dim)


def dot(a, b):
    return jnp.dot(a, b, preferred_element_type=f32)


def dot_t(a, b):
    return lax.dot_general(a, b, (((1,), (1,)), ((), ())), preferred_element_type=f32)


def split2(value):
    high = value.astype(bf16)
    return high, (value - high.astype(f32)).astype(bf16)


def split3(value):
    high = value.astype(bf16)
    rest = value - high.astype(f32)
    middle = rest.astype(bf16)
    return high, middle, (rest - middle.astype(f32)).astype(bf16)


def take(value, index):
    return jnp.take_along_axis(value, index, axis=1, mode="promise_in_bounds")


def row_of(ext):
    return jnp.where(ext < DEPTH, ext + OWN, jnp.where(ext < DEPTH + OWN, ext - DEPTH, ext))


def onehot(mask):
    return jnp.where(mask, 1.0, 0.0).astype(bf16)


def cycle_kernel(
    regions,
    disp_far, vel_far, mass_far, contact_far, modulus_far, stiff_far, level_far, window_far, conn_far,
    vel_out, disp_out, react_out, flag_out,
    disp_in, vel_in, mass_in, contact_in, modulus_in, stiff_in, level_in, window_in, conn_in,
    pack_out, pack_in, edge_out, edge_in, order_out, order_in, order_edge_out, order_edge_in,
    rim_out, rim_in, halo_out, halo_in,
    first_pay, first_a, first_b, pay, buf_a, buf_b, last_pay, last_a, last_b, react, disp_all,
    disp, vel, based, mass, contact, table, slot_cols, kron, tri,
    wab, back, conn_idx, half, perm, end1, end2, modulus, level, held, state,
    send_sem, recv_sem, pay_send, first_recv, a_recv, b_recv, load_sem, halo_send, halo_recv, last_recv,
):
    r = lax.axis_index("region")
    lane = lax.axis_index("lane")
    core = lax.rem(r, 2)
    chip = r // 2
    chips = regions // 2
    up = lax.rem(r + 1, regions)
    down = lax.rem(r + regions - 1, regions)
    size_a = 2 * LANES
    spot_a = lane * 2 + core
    dt = time_step
    node_total = regions * LANES * OWN * NB
    impactor_mass = impactor_ratio * node_total

    def peer_a(k):
        return (chip * 2 + lax.rem(k, 2), k // 2)

    def peer_b(k):
        return (k * 2 + core, lane)

    def signal(device):
        pl.semaphore_signal(
            pltpu.get_barrier_semaphore(), inc=1, device_id=device,
            device_id_type=pl.DeviceIdType.MESH,
        )

    def shifted(spot, step, size):
        return lax.rem(spot + step, size)

    @pl.loop(1, size_a)
    def _(k):
        signal(peer_a(shifted(spot_a, k, size_a)))

    @pl.loop(1, chips)
    def _(k):
        signal(peer_b(shifted(chip, k, chips)))

    @pl.when(lane == 0)
    def _():
        @pl.loop(0, LANES)
        def _(j):
            signal((down, j))

    @pl.when(lane == LANES - 1)
    def _():
        @pl.loop(0, LANES)
        def _(j):
            signal((up, j))

    def copy(src, dst, send, recv, device):
        return pltpu.make_async_remote_copy(
            src_ref=src, dst_ref=dst, send_sem=send, recv_sem=recv,
            device_id=device, device_id_type=pl.DeviceIdType.MESH,
        )

    def wait_bytes(ref, sem):
        pltpu.make_async_copy(ref, ref, sem).wait()

    loads = []
    for k, (far, here) in enumerate((
        (level_far, level_in), (window_far, window_in), (modulus_far, modulus_in),
        (conn_far, conn_in), (contact_far, contact_in), (mass_far, mass_in),
        (disp_far, disp_in), (vel_far, vel_in), (stiff_far, stiff_in),
    )):
        loads.append(pltpu.make_async_copy(far, here, load_sem.at[k]))
        loads[-1].start()
    for load in loads:
        load.wait()

    level_row = level_in[...].astype(f32)
    window_row = window_in[...].astype(f32)
    dest = iota((16, 64), 0)
    offsets = jnp.where(
        dest < LANES, (DEPTH - 1) - OWN * dest,
        jnp.where(dest == LANES, DEPTH - 1 - OWN * LANES, OWN + DEPTH - 1),
    ).astype(f32)
    anchor_all = window_row + offsets
    lowest = jnp.where(dest == LANES + 1, OWN + DEPTH - 1, 0).astype(f32)
    highest = jnp.where(dest == LANES, DEPTH - 1, ANCHORS - 1).astype(f32)
    wanted = jnp.where(
        (anchor_all >= lowest) & (anchor_all <= highest) & (dest < LANES + 2), 1.0, 0.0
    )
    before = onehot(iota((64, 64), 0) < iota((64, 64), 1))
    rank_key = jnp.where(wanted > 0.0, dot(wanted.astype(bf16), before), -1.0)
    count = jnp.sum(wanted, axis=1, keepdims=True)
    room = jnp.where(iota((16, 1), 0) < LANES, PACK, EDGE).astype(f32)
    overflow = jnp.max(jnp.where(count > room, 1.0, 0.0), axis=0, keepdims=True)
    picks = [
        onehot(iota((PACK, 64), 0).astype(f32) == rank_key[k : k + 1, :]) for k in range(LANES)
    ] + [
        onehot(iota((EDGE, 64), 0).astype(f32) == rank_key[k : k + 1, :])
        for k in (LANES, LANES + 1)
    ]
    pick = jnp.concatenate(picks, axis=0)
    conn_f = conn_in[...].astype(f32)
    block_data = jnp.concatenate(
        [modulus_in[...], level_row, window_row, jnp.zeros((NB - 18, 64), f32)], axis=0
    )
    chosen = sum(dot_t(pick, part) for part in split3(block_data))
    chosen_conn = dot(pick, conn_f.astype(bf16))
    for k in range(LANES):
        part = slice(k * PACK, (k + 1) * PACK)
        pack_out[k, :, :NB] = chosen_conn[part, :]
        pack_out[k, :, NB:] = chosen[part, :] + jnp.where(
            iota((PACK, NB), 1) == 17, float(DEPTH - 1 - OWN * k), 0.0
        )
    for k, offset in ((0, DEPTH - 1 - OWN * LANES), (1, OWN + DEPTH - 1)):
        part = slice(LANES * PACK + k * EDGE, LANES * PACK + (k + 1) * EDGE)
        edge_out[k, :, :NB] = chosen_conn[part, :]
        edge_out[k, :, NB:] = chosen[part, :] + jnp.where(
            iota((EDGE, NB), 1) == 17, float(offset), 0.0
        )

    def load_rim(rim_lane, first):
        for j in range(DEPTH):
            at = (rim_lane * OWN + first + j) * NB
            part = slice(at, at + NB)
            for c in range(3):
                rim_out[c, j : j + 1, :] = disp_in[c : c + 1, part]
                rim_out[3 + c, j : j + 1, :] = vel_in[c : c + 1, part]
        rows = slice(rim_lane * OWN + first, rim_lane * OWN + first + DEPTH)
        rim_out[6, :, :] = mass_in[rows, :]
        rim_out[7, :, :] = contact_in[rows, :]

    @pl.when(lane == 0)
    def _():
        load_rim(LANES - 1, OWN - DEPTH)

    @pl.when(lane == LANES - 1)
    def _():
        load_rim(0, 0)

    def load_nodes(place, source_lane, first, number):
        start = pl.multiple_of(source_lane * (OWN * NB), OWN * NB)
        for j in range(number):
            part = pl.ds(start + (first + j) * NB, NB)
            for c in range(3):
                disp[c, place + j : place + j + 1, :] = disp_in[c : c + 1, part]
                vel[c, place + j : place + j + 1, :] = vel_in[c : c + 1, part]
        rows = pl.ds(pl.multiple_of(source_lane * OWN, OWN), OWN)
        mass[place : place + number, :] = mass_in[rows, :][first : first + number, :]
        contact[place : place + number, :] = contact_in[rows, :][first : first + number, :]

    left_row, right_row = OWN, OWN + DEPTH
    disp[...] = jnp.zeros_like(disp)
    vel[...] = jnp.zeros_like(vel)
    mass[...] = jnp.ones_like(mass)
    contact[...] = jnp.zeros_like(contact)
    load_nodes(0, lane, 0, OWN)
    load_nodes(left_row, jnp.maximum(lane - 1, 0), OWN - DEPTH, DEPTH)
    load_nodes(right_row, jnp.minimum(lane + 1, LANES - 1), 0, DEPTH)

    own = pl.ds(0, OWN)
    own_contact = contact[own, :]
    own_mass = mass[own, :]
    push_rate = (dt * dt * contact_stiffness) * own_contact / own_mass
    sums = [
        jnp.sum(own_contact * (start_gap - disp[0, own, :]), axis=0, keepdims=True),
        jnp.sum(own_contact, axis=0, keepdims=True),
        jnp.sum(own_contact * push_rate, axis=0, keepdims=True),
    ]
    first_pay[...] = jnp.concatenate(sums, axis=0)
    first_a[spot_a] = first_pay[...]

    pl.semaphore_wait(pltpu.get_barrier_semaphore(), size_a - 1 + chips - 1 + 2)

    @pl.loop(1, size_a)
    def _(k):
        copy(
            first_pay, first_a.at[spot_a], pay_send.at[0], first_recv.at[0],
            peer_a(shifted(spot_a, k, size_a)),
        ).start()

    edge_up = copy(edge_out.at[0], edge_in.at[lane], send_sem.at[0], recv_sem.at[0], (up, 0))
    edge_down = copy(
        edge_out.at[1], edge_in.at[lane], send_sem.at[1], recv_sem.at[0], (down, LANES - 1)
    )
    edge_up.start()
    edge_down.start()

    @pl.loop(1, LANES)
    def _(k):
        there = shifted(lane, k, LANES)
        copy(
            pack_out.at[there], pack_in.at[lane], send_sem.at[3], recv_sem.at[2], (r, there)
        ).start()

    rim_up = copy(rim_out, rim_in, send_sem.at[2], recv_sem.at[1], (up, 0))
    rim_down = copy(rim_out, rim_in, send_sem.at[2], recv_sem.at[1], (down, LANES - 1))

    @pl.when(lane == 0)
    def _():
        rim_up.start()

    @pl.when(lane == LANES - 1)
    def _():
        rim_down.start()

    pack_in[lane] = pack_out[lane]

    lane64 = iota((64, NB), 1)
    keys = conn_f * float(NB) + lane64.astype(f32)
    span = 2
    while span <= NB:
        step = span // 2
        while step >= 1:
            other = take(keys, lane64 ^ step)
            keep_low = ((lane64 & step) == 0) == ((lane64 & span) == 0)
            keys = jnp.where(keep_low, jnp.minimum(keys, other), jnp.maximum(keys, other))
            step //= 2
        span *= 2
    order = (keys.astype(i32) & (NB - 1)).astype(f32)
    chosen_order = dot(pick, order.astype(bf16))
    for k in range(LANES):
        order_out[k] = chosen_order[k * PACK : (k + 1) * PACK, :]
    for k in range(2):
        start = LANES * PACK + k * EDGE
        order_edge_out[k] = chosen_order[start : start + EDGE, :]
    order_up = copy(
        order_edge_out.at[0], order_edge_in.at[lane], send_sem.at[7], recv_sem.at[6], (up, 0)
    )
    order_down = copy(
        order_edge_out.at[1], order_edge_in.at[lane], send_sem.at[8], recv_sem.at[6],
        (down, LANES - 1),
    )
    order_up.start()
    order_down.start()

    @pl.loop(1, LANES)
    def _(k):
        there = shifted(lane, k, LANES)
        copy(
            order_out.at[there], order_in.at[lane], send_sem.at[4], recv_sem.at[3], (r, there)
        ).start()

    order_in[lane] = order_out[lane]

    stiff = split2(stiff_in[...])
    at = iota((3 * NB, 24), 0)
    names = onehot((at // NB) * 8 + lax.rem(at, 8) == iota((3 * NB, 24), 1))
    row_element = lax.rem(iota((3 * NB, 3 * NB), 0), NB) // 8
    col_element = lax.rem(iota((3 * NB, 3 * NB), 1), NB) // 8
    same = row_element == col_element
    for part, places in ((stiff[0], (0, 1)), (stiff[1], (2,))):
        grown = dot_t(dot_t(names, part).astype(bf16), names)
        grown = jnp.where(same, grown, 0.0).astype(bf16)
        for at_place in places:
            kron[at_place * 3 * NB : (at_place + 1) * 3 * NB, :] = grown
    running = onehot(iota((NB, NB), 0) <= iota((NB, NB), 1))
    tri[0:NB, :] = running
    tri[NB:, :] = running

    @pl.when((lane != 0) & (lane != LANES - 1))
    def _():
        edge_in[...] = jnp.zeros_like(edge_in)
        order_edge_in[...] = jnp.zeros_like(order_edge_in)

    wait_bytes(first_a.at[pl.ds(0, size_a - 1)], first_recv.at[0])
    total = first_a[0]
    for k in range(1, size_a):
        total = total + first_a[k]
    first_b[chip] = total
    first_pay2 = first_b.at[chip]

    @pl.loop(1, chips)
    def _(k):
        copy(
            first_pay2, first_b.at[chip], pay_send.at[1], first_recv.at[1],
            peer_b(shifted(chip, k, chips)),
        ).start()

    @pl.when((lane == 0) | (lane == LANES - 1))
    def _():
        wait_bytes(edge_in, recv_sem.at[0])
        wait_bytes(rim_in, recv_sem.at[1])

    def unpack_rim(place):
        for c in range(3):
            disp[c, place : place + DEPTH, :] = rim_in[c]
            vel[c, place : place + DEPTH, :] = rim_in[3 + c]
        mass[place : place + DEPTH, :] = rim_in[6]
        contact[place : place + DEPTH, :] = rim_in[7]

    @pl.when(lane == 0)
    def _():
        unpack_rim(left_row)

    @pl.when(lane == LANES - 1)
    def _():
        unpack_rim(right_row)

    wait_bytes(pack_in.at[pl.ds(0, LANES - 1)], recv_sem.at[2])

    offered = LANES * (PACK + EDGE)
    rows_in = jnp.concatenate(
        [pack_in[...].reshape(LANES * PACK, 2 * NB), edge_in[...].reshape(LANES * EDGE, 2 * NB)],
        axis=0,
    )
    data_in = rows_in[:, NB:]
    data_parts = split3(data_in)
    looked = onehot(iota((8, NB), 1) == 16)
    present = jnp.where(dot_t(looked, data_parts[0]) > 0.0, 1.0, 0.0)
    strict = onehot(iota((offered, offered), 0) < iota((offered, offered), 1))
    key = jnp.where(present > 0.0, dot(present.astype(bf16), strict), -1.0)[0:1, :]
    taken = jnp.sum(present[0:1, :], axis=1, keepdims=True)
    overflow = jnp.maximum(overflow, jnp.where(taken > float(ROWS), 1.0, 0.0))
    keep = onehot(iota((ROWS, offered), 0).astype(f32) == key)
    conn = dot(keep, rows_in[:, :NB].astype(bf16))
    data = dot(keep, data_parts[0]) + dot(keep, data_parts[1]) + dot(keep, data_parts[2])

    lane_no = iota((ROWS, NB), 1)
    modulus[...] = take(data, lane_no // 8)
    level[...] = take(data, jnp.full((ROWS, NB), 16, i32)).astype(i32) - 1
    anchor = take(data, jnp.full((ROWS, NB), 17, i32)).astype(i32)
    wab[:ROWS, :] = onehot((lane_no & 31) == row_of(anchor))
    wab[ROWS:, :] = onehot((lane_no & 31) == row_of(anchor + 1))
    named = dot_t(onehot(iota((8, NB), 1) == 17), data.astype(bf16))
    anchor_row = named[0:1, :].astype(i32)
    node_row = iota((NODE_ROWS, ROWS), 0)
    back_a = onehot(node_row == row_of(anchor_row))
    back_b = onehot(node_row == row_of(anchor_row + 1))
    back[...] = jnp.concatenate([back_a, back_b, back_a, back_b], axis=1)
    conn_i = conn.astype(i32)
    conn_idx[...] = conn_i & (NB - 1)
    half[...] = conn_i >> 7

    @pl.when((lane == 0) | (lane == LANES - 1))
    def _():
        wait_bytes(order_edge_in, recv_sem.at[6])

    wait_bytes(order_in.at[pl.ds(0, LANES - 1)], recv_sem.at[3])
    order_rows = jnp.concatenate(
        [
            order_in[...].reshape(LANES * PACK, NB),
            order_edge_in[...].reshape(LANES * EDGE, NB),
        ],
        axis=0,
    )
    order = dot(keep, order_rows.astype(bf16)).astype(i32)
    perm[...] = order
    nodes = take(conn_i, order)
    for ref, base in ((end1, 0), (end2, NB)):
        target = lane_no + base
        found = jnp.zeros((ROWS, NB), i32)
        for step in (64, 32, 16, 8, 4, 2, 1, 0):
            probe = take(nodes, found + (step - 1 if step else 0))
            found = jnp.where(probe <= target, found + max(step, 1), found)
        ref[...] = found - 1

    held[...] = jnp.zeros_like(held)
    table[...] = jnp.zeros_like(table)

    zero_row = jnp.zeros((1, NB), f32)
    state[0:1, :] = zero_row + start_gap
    state[1:2, :] = zero_row + start_gap
    state[5:6, :] = jnp.where(overflow > 0.0, jnp.inf, 0.0) + zero_row

    def collect_first():
        wait_bytes(first_b.at[pl.ds(0, chips - 1)], first_recv.at[1])
        total = first_b[0]
        for k in range(1, chips):
            total = total + first_b[k]
        first = jnp.sum(total, axis=1, keepdims=True)
        reaction = first[0:1, :] + zero_row
        speed = start_speed - dt * contact_stiffness * reaction / impactor_mass
        state[1:2, :] = start_gap + dt * speed
        state[2:3, :] = speed
        state[3:4, :] = first[1:2, :] + zero_row
        state[4:5, :] = first[2:3, :] + zero_row
        react[0:1, :] = reaction / node_total

    first_lane = iota((ROWS, NB), 1) == 0

    def to_slots(fields):
        width = len(fields) * NB
        parts = [split3(field) for field in fields]
        for k in range(3):
            table[32 * k : 32 * k + NODE_ROWS, :width] = jnp.concatenate(
                [part[k] for part in parts], axis=1
            )
        both = dot(wab[...], table[:, :width])
        index = conn_idx[...]
        second = half[...] > 0
        slots = []
        for c in range(len(fields)):
            cols = slice(c * NB, (c + 1) * NB)
            slots.append(
                jnp.where(second, take(both[ROWS:, cols], index), take(both[:ROWS, cols], index))
            )
        return slots

    def forces(s):
        top, rest = split2(jnp.concatenate(to_slots([disp[c] for c in range(3)]), axis=1))
        strain = dot(jnp.concatenate([top, rest, top], axis=1), kron[...])
        active = (level[...] & s) == 0
        order = perm[...]
        mod = modulus[...]
        sorted_forces = []
        for c in range(3):
            g = strain[:, c * NB : (c + 1) * NB]
            fresh = mod * (g + hardening * g * g * g)
            now = jnp.where(active, fresh, held[c])
            held[c] = now
            sorted_forces.append(jnp.concatenate(split2(take(now, order)), axis=1))
        sums = dot(jnp.concatenate(sorted_forces, axis=0), tri[...])
        e1 = end1[...]
        e2 = end2[...]
        for c in range(3):
            part = sums[c * ROWS : (c + 1) * ROWS, :]
            upto1 = jnp.where(e1 >= 0, take(part, e1 & (NB - 1)), 0.0)
            upto2 = jnp.where(e2 >= 0, take(part, e2 & (NB - 1)), 0.0)
            prev1 = pltpu.roll(upto1, 1, 1)
            prev2 = pltpu.roll(upto2, 1, 1)
            f1 = split2(upto1 - jnp.where(first_lane, 0.0, prev1))
            f2 = split2(upto2 - jnp.where(first_lane, prev1, prev2))
            cols = slice(c * NB, (c + 1) * NB)
            slot_cols[0:ROWS, cols] = f1[0]
            slot_cols[ROWS : 2 * ROWS, cols] = f2[0]
            slot_cols[2 * ROWS : 3 * ROWS, cols] = f1[1]
            slot_cols[3 * ROWS :, cols] = f2[1]
        return dot(back[...], slot_cols[...])

    ahead = SUBSTEPS - 2

    def sum_ahead():
        centre = state[1:2, :]
        state[6:7, :] = centre
        weight = contact[...]
        inverse = 1.0 / mass[...]
        rate = (dt * contact_stiffness) * weight * inverse
        push = dt * rate
        start_vel = based[0] + centre * rate
        start_disp = [disp[0] + dt * start_vel] + [disp[c] + dt * based[c] for c in (1, 2)]
        owned = iota((NODE_ROWS, NB), 0) < OWN
        share = jnp.where(owned, dt * dt * weight * inverse, 0.0)
        slots = to_slots(start_disp + [push, share])
        top, rest = split2(jnp.concatenate(slots[:3], axis=1))
        g0 = dot(jnp.concatenate([top, rest, top], axis=1), kron[:, :NB])
        top, rest = split2(slots[3])
        first_block = jnp.concatenate(
            [kron[k * 3 * NB : k * 3 * NB + NB, :NB] for k in range(3)], axis=0
        )
        g1 = dot(jnp.concatenate([top, rest, top], axis=1), first_block)
        active = (level[...] & ahead) == 0
        scale = slots[4] * modulus[...]
        scale = jnp.where(active, scale, 0.0)
        kept = jnp.where(active, 0.0, slots[4] * held[0])
        terms = [
            kept + scale * (g0 + hardening * g0 * g0 * g0),
            scale * (g1 + 3.0 * hardening * g0 * g0 * g1),
            scale * (3.0 * hardening) * g0 * g1 * g1,
            scale * hardening * g1 * g1 * g1,
        ]
        nodal = [
            jnp.where(
                owned, weight * (start_gap - start_disp[0] - dt * start_vel + push * start_disp[0]), 0.0
            ),
            jnp.where(owned, weight * push * (push - 2.0), 0.0),
        ]
        rows = [jnp.sum(term, axis=0, keepdims=True) for term in terms]
        rows[0] = rows[0] + jnp.sum(nodal[0], axis=0, keepdims=True) + state[5:6, :]
        rows[1] = rows[1] + jnp.sum(nodal[1], axis=0, keepdims=True)
        last_pay[...] = jnp.concatenate(rows, axis=0)
        last_a[spot_a] = last_pay[...]

        @pl.loop(1, size_a)
        def _(k):
            copy(
                last_pay, last_a.at[spot_a], pay_send.at[4], last_recv.at[0],
                peer_a(shifted(spot_a, k, size_a)),
            ).start()

    def relay_last():
        wait_bytes(last_a.at[pl.ds(0, size_a - 1)], last_recv.at[0])
        value = last_a[0]
        for k in range(1, size_a):
            value = value + last_a[k]
        last_b[chip] = value

        @pl.loop(1, chips)
        def _(k):
            copy(
                last_b.at[chip], last_b.at[chip], pay_send.at[5], last_recv.at[1],
                peer_b(shifted(chip, k, chips)),
            ).start()

    def collect_last():
        wait_bytes(last_b.at[pl.ds(0, chips - 1)], last_recv.at[1])
        value = last_b[0]
        for k in range(1, chips):
            value = value + last_b[k]
        total = jnp.sum(value, axis=1, keepdims=True) + jnp.zeros((4, NB), f32)
        shift = state[7:8, :] - state[6:7, :]
        cubic = total[0:1] + shift * (total[1:2] + shift * (total[2:3] + shift * total[3:4]))
        reaction = (
            cubic + (state[1:2, :] - start_gap) * state[3:4, :] - state[0:1, :] * state[4:5, :]
        )
        react[SUBSTEPS - 1 :, :] = reaction / node_total

    def relay(s):
        wait_bytes(buf_a.at[s, pl.ds(0, size_a - 1)], a_recv.at[s])
        value = buf_a[s, 0]
        for k in range(1, size_a):
            value = value + buf_a[s, k]
        buf_b[s, chip] = value

        @pl.loop(1, chips)
        def _(k):
            copy(
                buf_b.at[s, chip], buf_b.at[s, chip], pay_send.at[3], b_recv.at[s],
                peer_b(shifted(chip, k, chips)),
            ).start()

    def collect(s):
        wait_bytes(buf_b.at[s, pl.ds(0, chips - 1)], b_recv.at[s])
        value = buf_b[s, 0]
        for k in range(1, chips):
            value = value + buf_b[s, k]
        total = jnp.sum(value, axis=1, keepdims=True) + zero_row
        before_z = state[0:1, :]
        now_z = state[1:2, :]
        reaction = total + (now_z - start_gap) * state[3:4, :] - before_z * state[4:5, :]
        react[pl.ds(s + 1, 1), :] = reaction / node_total
        speed = state[2:3, :] - dt * contact_stiffness * reaction / impactor_mass
        state[0:1, :] = now_z
        state[1:2, :] = now_z + dt * speed
        state[2:3, :] = speed

    left = (jnp.where(lane == 0, down, r), lax.rem(lane + LANES - 1, LANES))
    right = (jnp.where(lane == LANES - 1, up, r), lax.rem(lane + 1, LANES))

    def halo_copies(turn):
        return [
            copy(
                halo_out.at[turn, side], halo_in.at[turn, 1 - side],
                halo_send.at[turn, side], halo_recv.at[turn, 1 - side], there,
            )
            for side, there in ((0, left), (1, right))
        ]

    def substep(s):
        force = forces(s)
        since = lax.rem(s, DEPTH)
        row_no = iota((NODE_ROWS, NB), 0)
        ext_no = jnp.where(
            row_no < OWN, row_no + DEPTH, jnp.where(row_no < OWN + DEPTH, row_no - OWN, row_no)
        )
        margin = jnp.where(since == DEPTH - 1, 0, 1 + since)
        valid = (ext_no >= margin) & (ext_no < OWN + 2 * DEPTH - margin)
        weight = contact[...]
        inverse = 1.0 / mass[...]
        for c in range(3):
            pull = -force[:, c * NB : (c + 1) * NB]
            if c == 0:
                pull = pull - contact_stiffness * weight * disp[0]
            based[c] = vel[c] + dt * (pull * inverse)
        free = disp[0, own, :] + dt * based[0, own, :]
        part = jnp.sum(contact[own, :] * (start_gap - free), axis=0, keepdims=True)
        pay[s] = part + state[5:6, :]
        buf_a[s, spot_a] = pay[s]

        @pl.when(s < ahead)
        def _():
            @pl.loop(1, size_a)
            def _(k):
                copy(
                    pay.at[s], buf_a.at[s, spot_a], pay_send.at[2], a_recv.at[s],
                    peer_a(shifted(spot_a, k, size_a)),
                ).start()

        @pl.when((s == 2) | (s == 5))
        def _():
            turn = s // DEPTH
            for side, first in ((0, 0), (1, OWN - DEPTH)):
                for c in range(3):
                    halo_out[turn, side, c] = disp[c, first : first + DEPTH, :]
                    halo_out[turn, side, 3 + c] = based[c, first : first + DEPTH, :]
            moves = halo_copies(turn)
            for move in moves:
                move.start()

            @pl.loop(0, 3)
            def _(k):
                relay(s - 2 + k)

            for move in moves:
                move.wait_recv()
            for side, place in ((0, left_row), (1, right_row)):
                for c in range(3):
                    disp[c, place : place + DEPTH, :] = halo_in[turn, side, c]
                    based[c, place : place + DEPTH, :] = halo_in[turn, side, 3 + c]

        @pl.when(s == ahead - 1)
        def _():
            sum_ahead()

        @pl.when(s == 1)
        def _():
            collect_first()

        @pl.when(s >= 2)
        def _():
            collect(s - 2)

        @pl.when(s == ahead - 1)
        def _():
            state[7:8, :] = state[1:2, :]

        z_now = state[1:2, :]
        pushed = (dt * contact_stiffness) * z_now * (weight * inverse)
        for c in range(3):
            fresh = based[c] + pushed if c == 0 else based[c]
            vel[c] = jnp.where(valid, fresh, vel[c])
            disp[c] = jnp.where(valid, disp[c] + dt * fresh, disp[c])

    own_part = pl.ds(pl.multiple_of(lane * (OWN * NB), OWN * NB), OWN * NB)
    other_parts = pl.ds(0, (LANES - 1) * OWN * NB)

    def gather_out(source, ref, slot):
        start = pl.multiple_of(lane * (OWN * NB), OWN * NB)
        for j in range(OWN):
            for c in range(3):
                ref[c : c + 1, pl.ds(start + j * NB, NB)] = source[c, j : j + 1, :]

        @pl.loop(1, LANES)
        def _(k):
            there = (r, shifted(lane, k, LANES))
            copy(
                ref.at[:, own_part], ref.at[:, own_part], send_sem.at[5 + slot],
                recv_sem.at[4 + slot], there,
            ).start()

    @pl.loop(0, SUBSTEPS)
    def _(s):
        substep(s)

        @pl.when(s == SUBSTEPS - 2)
        def _():
            gather_out(disp, disp_all, 0)

    gather_out(vel, vel_out, 1)
    relay_last()
    wait_bytes(disp_all.at[:, other_parts], recv_sem.at[4])
    for s in range(SUBSTEPS - 1):
        react_out[s] = jnp.max(react[s : s + 1, :])
    wait_bytes(vel_out.at[:, other_parts], recv_sem.at[5])
    disp_out[...] = disp_all[...] + dt * vel_out[...]
    collect_last()
    react_out[SUBSTEPS - 1] = jnp.max(react[SUBSTEPS - 1 :, :])
    flag_out[0] = jnp.max(jnp.where(jnp.abs(react[...]) < jnp.inf, 0, 1))

    edge_up.wait_send()
    edge_down.wait_send()

    @pl.when((lane == 0) | (lane == LANES - 1))
    def _():
        rim_up.wait_send()

    order_up.wait_send()
    order_down.wait_send()
    for turn in range(2):
        for move in halo_copies(turn):
            move.wait_send()
    wait_bytes(pack_in.at[pl.ds(0, LANES - 1)], send_sem.at[3])
    wait_bytes(order_in.at[pl.ds(0, LANES - 1)], send_sem.at[4])
    wait_bytes(disp_all.at[:, other_parts], send_sem.at[5])
    wait_bytes(vel_out.at[:, other_parts], send_sem.at[6])
    wait_bytes(first_a.at[pl.ds(0, size_a - 1)], pay_send.at[0])
    wait_bytes(first_b.at[pl.ds(0, chips - 1)], pay_send.at[1])
    wait_bytes(buf_a.at[pl.ds(0, ahead), pl.ds(0, size_a - 1)], pay_send.at[2])
    wait_bytes(buf_b.at[pl.ds(0, ahead), pl.ds(0, chips - 1)], pay_send.at[3])
    wait_bytes(last_a.at[pl.ds(0, size_a - 1)], pay_send.at[4])
    wait_bytes(last_b.at[pl.ds(0, chips - 1)], pay_send.at[5])


def run_cycle(regions, init_disp, init_vel, mass, contact, modulus, stiffness, levels, windows, conn):
    chips = regions // 2
    vmem = pl.BlockSpec(memory_space=pltpu.VMEM)
    V = pltpu.VMEM
    vel, disp, react, flag = pl.pallas_call(
        functools.partial(cycle_kernel, regions),
        out_shape=(
            jax.ShapeDtypeStruct(init_vel.shape, f32),
            jax.ShapeDtypeStruct(init_disp.shape, f32),
            jax.ShapeDtypeStruct((SUBSTEPS,), f32),
            jax.ShapeDtypeStruct((1,), i32),
        ),
        in_specs=[pl.BlockSpec(memory_space=pl.ANY)] * 9,
        out_specs=[vmem] * 2 + [pl.BlockSpec(memory_space=pltpu.SMEM)] * 2,
        scratch_shapes=[
            V(init_disp.shape, f32), V(init_vel.shape, f32), V((LANES * OWN, NB), f32),
            V((LANES * OWN, NB), f32), V((16, 64), f32), V((24, 24), f32),
            V((1, 64), i32), V((1, 64), i32), V((64, NB), i32),
            V((LANES, PACK, 2 * NB), f32), V((LANES, PACK, 2 * NB), f32),
            V((2, EDGE, 2 * NB), f32), V((LANES, EDGE, 2 * NB), f32),
            V((LANES, PACK, NB), f32), V((LANES, PACK, NB), f32),
            V((2, EDGE, NB), f32), V((LANES, EDGE, NB), f32),
            V((8, DEPTH, NB), f32), V((8, DEPTH, NB), f32),
            V((2, 2, 6, DEPTH, NB), f32), V((2, 2, 6, DEPTH, NB), f32),
            V((3, NB), f32), V((2 * LANES, 3, NB), f32), V((chips, 3, NB), f32),
            V((SUBSTEPS, 1, NB), f32), V((SUBSTEPS, 2 * LANES, 1, NB), f32),
            V((SUBSTEPS, chips, 1, NB), f32),
            V((4, NB), f32), V((2 * LANES, 4, NB), f32), V((chips, 4, NB), f32),
            V((SUBSTEPS, NB), f32), V(init_disp.shape, f32),
            V((3, NODE_ROWS, NB), f32), V((3, NODE_ROWS, NB), f32), V((3, NODE_ROWS, NB), f32),
            V((NODE_ROWS, NB), f32), V((NODE_ROWS, NB), f32),
            V((NB, 5 * NB), bf16), V((4 * ROWS, 3 * NB), bf16),
            V((9 * NB, 3 * NB), bf16), V((2 * NB, NB), bf16),
            V((2 * ROWS, NB), bf16), V((NODE_ROWS, 4 * ROWS), bf16),
            V((ROWS, NB), i32), V((ROWS, NB), i32), V((ROWS, NB), i32),
            V((ROWS, NB), i32), V((ROWS, NB), i32),
            V((ROWS, NB), f32), V((ROWS, NB), i32), V((3, ROWS, NB), f32), V((8, NB), f32),
            pltpu.SemaphoreType.DMA((9,)), pltpu.SemaphoreType.DMA((7,)),
            pltpu.SemaphoreType.DMA((6,)), pltpu.SemaphoreType.DMA((2,)),
            pltpu.SemaphoreType.DMA((SUBSTEPS,)), pltpu.SemaphoreType.DMA((SUBSTEPS,)),
            pltpu.SemaphoreType.DMA((9,)),
            pltpu.SemaphoreType.DMA((2, 2)), pltpu.SemaphoreType.DMA((2, 2)),
            pltpu.SemaphoreType.DMA((2,)),
        ],
        compiler_params=pltpu.CompilerParams(
            collective_id=0, has_side_effects=True, vmem_limit_bytes=48 * 1024 * 1024
        ),
        name="crush_cycle",
    )(
        init_disp, init_vel, mass.reshape(-1, NB), contact.reshape(-1, NB), modulus.T, stiffness,
        levels.reshape(1, -1), windows.reshape(1, -1), conn,
    )
    return (disp, vel, react), flag[0]


def sum_over(value, axis):
    count = lax.axis_size(axis)
    step = 1
    while step < count:
        value = value + lax.ppermute(value, axis, [(i, i ^ step) for i in range(count)])
        step *= 2
    return value


def with_halo(array, sides, width):
    for axis, dim in sides:
        count, length = (lax.axis_size(axis), array.shape[dim])
        up = [(i, (i + 1) % count) for i in range(count)]
        down = [(j, i) for i, j in up]
        last = lax.slice_in_dim(array, length - width, length, axis=dim)
        initial = lax.slice_in_dim(array, 0, width, axis=dim)
        before = lax.ppermute(last, axis, up)
        after = lax.ppermute(initial, axis, down)
        array = jnp.concatenate([before, array, after], axis=dim)
    return array


def element_forces(slot_disp, block_modulus, stiffness):
    count = slot_disp.shape[0]
    elements = block_modulus.shape[1]
    vectors = (
        slot_disp.reshape(count, 3, elements, 8).transpose(0, 2, 1, 3).reshape(count, elements, 24)
    )
    strain = jnp.einsum("bek,jk->bej", vectors, stiffness, precision=lax.Precision.HIGHEST)
    result = block_modulus[:, :, None] * (strain + hardening * strain * strain * strain)
    return (
        result.reshape(count, elements, 3, 8).transpose(0, 2, 1, 3).reshape(count, 3, elements * 8)
    )


def plain_cycle(init_disp, init_vel, mass, contact, modulus, stiffness, levels, windows, conn):
    region_count = lax.axis_size("region")
    node_region = init_disp.shape[1]
    slot_count = conn.shape[1]
    block_rows = NB
    node_total = node_region * region_count
    impactor_mass = impactor_ratio * node_total
    extended_blocks = node_region // block_rows + 2
    block_order = jnp.argsort(levels, stable=True)
    conn = conn[block_order]
    windows = windows[block_order]
    levels = levels[block_order]
    modulus = modulus[block_order]
    level_slot = (
        (levels >= 2).astype(jnp.int32)
        + (levels >= 4).astype(jnp.int32)
        + (levels >= 8).astype(jnp.int32)
    )
    level_force = jnp.zeros((4, 3, extended_blocks, block_rows), jnp.float32)
    disp_full = init_disp
    disp_state = init_disp
    vel_state = init_vel
    gap_now = jnp.float32(start_gap)
    speed = jnp.float32(start_speed)
    history = []
    slot_iota = lax.broadcasted_iota(jnp.int32, (group_size, 2 * block_rows, slot_count), 1)
    for substep in range(SUBSTEPS):
        top_level = SUBSTEPS if substep == 0 else min(substep & -substep, SUBSTEPS)
        top_index = top_level.bit_length() - 1
        active_count = jnp.sum((levels <= top_level).astype(jnp.int32))
        level_force = level_force.at[: top_index + 1].set(0.0)
        disp_ext = with_halo(disp_full, (("region", 1),), block_rows)

        def one_group(group_index, totals):
            offset = group_index * group_size
            conn_group = lax.dynamic_slice_in_dim(conn, offset, group_size, 0)
            window_group = lax.dynamic_slice_in_dim(windows, offset, group_size, 0)
            level_group = lax.dynamic_slice_in_dim(level_slot, offset, group_size, 0)
            modulus_group = lax.dynamic_slice_in_dim(modulus, offset, group_size, 0)
            valid = offset + jnp.arange(group_size, dtype=jnp.int32) < active_count
            window_disp = jax.vmap(
                lambda first_block: lax.dynamic_slice_in_dim(
                    disp_ext, first_block * block_rows, 2 * block_rows, 1
                )
            )(window_group)
            onehot = (slot_iota == conn_group[:, None, :]).astype(jnp.float32)
            slot_disp = jnp.einsum(
                "gcw,gws->gcs", window_disp, onehot, precision=lax.Precision.HIGHEST
            )
            slot_force = element_forces(slot_disp, modulus_group, stiffness)
            slot_force = jnp.where(valid[:, None, None], slot_force, 0.0)
            window_force = jnp.einsum(
                "gcs,gws->gcw", slot_force, onehot, precision=lax.Precision.HIGHEST
            )
            window_force = window_force.reshape(group_size, 3, 2, block_rows)
            totals = totals.at[level_group, :, window_group].add(window_force[:, :, 0])
            totals = totals.at[level_group, :, window_group + 1].add(window_force[:, :, 1])
            return totals

        group_total = (active_count + group_size - 1) // group_size
        level_force = lax.fori_loop(0, group_total, one_group, level_force)
        force_ext = jnp.sum(level_force, axis=0).reshape(3, extended_blocks * block_rows)
        outer_rims = jnp.concatenate(
            (force_ext[:, :block_rows], force_ext[:, -block_rows:]), axis=1
        )
        rim_terms = with_halo(outer_rims, (("region", 1),), block_rows)
        partial_force = force_ext[:, block_rows:-block_rows]
        partial_force = partial_force.at[:, :block_rows].add(rim_terms[:, :block_rows])
        partial_force = partial_force.at[:, -block_rows:].add(rim_terms[:, -block_rows:])
        force = sum_over(partial_force, "lane")
        disp_state = disp_full
        gap = gap_now - disp_state[0]
        total = sum_over(jnp.sum(contact * gap), "region")
        history.append(total / node_total)
        push = jnp.zeros_like(force).at[0].set(contact_stiffness * contact * gap)
        accel = (push - force) / mass[None, :]
        vel_state = vel_state + time_step * accel
        disp_state = disp_state + time_step * vel_state
        speed = speed - time_step * contact_stiffness * total / impactor_mass
        gap_now = gap_now + time_step * speed
        disp_full = disp_state
    return (disp_full, vel_state, jnp.stack(history))


def on_device(*arguments):
    regions = lax.axis_size("region")
    fast, flag = run_cycle(regions, *arguments)
    return lax.cond(flag == 0, lambda: fast, lambda: plain_cycle(*arguments))


def solution(mesh):
    in_specs = (
        P(None, "region"),
        P(None, "region"),
        P("region"),
        P("region"),
        P(("region", "lane"), None),
        P(),
        P(("region", "lane")),
        P(("region", "lane")),
        P(("region", "lane"), None),
    )
    out_specs = (P(None, "region"), P(None, "region"), P())
    return jax.shard_map(
        on_device, mesh=mesh, in_specs=in_specs, out_specs=out_specs, check_vma=False
    )
```

time: 80.6 us -> 72.4 us (0.90)
  Pallas kernels: 76.5 us -> 67.9 us
  local copies, waits for them, and re-layouts: 1.4 us -> 2.53 us
  other arithmetic: 0.85 us -> 0 us
    pallas_call x1, Pallas kernels: 76.5 us -> 67.9 us  [run_cycle(): pl.pallas_call(functools.partial(cycle_kernel, regions), out_shape=(jax.S...]
    unnamed x18 -> x21, local copies, waits for them, and re-layouts: 0.78 us -> 2.53 us
    add x1 -> x0, other arithmetic: 0.85 us -> none  [run_cycle(): disp.transpose(1, 0, 2, 3).reshape(3, -1) + time_step * velocity]
where the time goes in v3:
time: 72.4 us; the launch traced here: 72.1 us
  Pallas kernels  67.9 us (94%)
  local copies, waits for them, and re-layouts  2.53 us (3%)
  between operations  1.46 us (2%)
    pallas_call x1, Pallas kernels, run_cycle(): pl.pallas_call(functools.partial(cycle_kernel, regions), out_shape=(jax.S...  67.9 us
    unnamed x21, local copies, waits for them, and re-layouts  2.53 us

profile of v3, /device:TPU:1, one launch (start us, length us, event | category | flops | bytes accessed | tf_op | source)
XLA Modules:
  0.0 72.1 jit_solution(18245944045904343074)
XLA Ops:
  0.6 0.0 copy-start.8
  0.6 0.0 copy-start
  0.7 0.0 copy-start.1
  0.7 0.7 copy-done.8
  1.3 0.0 copy-done
  1.3 0.0 copy-done.1
  1.3 0.0 copy-start.3
  1.3 0.0 copy-start.4
  1.3 0.0 copy-start.5
  1.4 0.0 copy-start.6
  1.4 0.0 copy-start.7
  1.4 67.9 %crush_cycle.1 = (f32[3,8192]{1,0:T(4,128)S(1)}, f32[3,8192]{1,0:T(4,128)S(1)}, f32[8]{0:T(128)S(1)}, s32[1]{0:T(128)}) custom-call(f32[3,8192]{1,0:T(4,128)} %disp_far.1, f32[3,8192]{1,0:T(4,128)} %vel_far.1, f32[64,128]{1,0:T(8,128)} %bitcast.665, f32[64,128]{1,0:T(8,128)} %bitcast.664, f32[16,64]{1,0:T(8,128)S(1)} %bitcast.722, f32[24,24]{1,0:T(8,128)} %stiff_far.1, ...), custom_call_target="tpu_custom_call" | custom-call | tf_op jit(solution)/shard_map/crush_cycle/pallas_call | solution.py:758
  69.3 0.0 copy-start.2
  70.0 0.0 copy-done.3
  70.0 0.0 copy-done.4
  70.0 0.0 copy-done.5
  70.0 0.0 copy-done.6
  70.1 0.0 copy-done.7
  70.1 0.0 copy-done.2
  70.1 0.2 conditional.1
  70.3 0.7 copy.630
  71.0 0.7 copy.631
  71.6 0.5 copy.632
Async XLA Ops:
  0.6 0.7 copy-start.8
  0.6 0.7 copy-start
  0.7 0.7 copy-start.1
  1.3 68.7 %copy-start.3 = (f32[8192]{0:T(1024)S(1)}, f32[8192]{0:T(1024)}, u32[]{:S(2)}) copy-start(f32[8192]{0:T(1024)} %param.99) | copy-start | bytes 98308
  1.3 68.7 %copy-start.4 = (s32[64,128]{1,0:T(8,128)S(1)}, s32[64,128]{1,0:T(8,128)}, u32[]{:S(2)}) copy-start(s32[64,128]{1,0:T(8,128)} %conn_far.1) | copy-start | bytes 98308
  1.3 68.7 %copy-start.5 = (f32[8192]{0:T(1024)S(1)}, f32[8192]{0:T(1024)}, u32[]{:S(2)}) copy-start(f32[8192]{0:T(1024)} %param.98) | copy-start | bytes 98308
  1.4 68.7 %copy-start.6 = (f32[3,8192]{1,0:T(4,128)S(1)}, f32[3,8192]{1,0:T(4,128)}, u32[]{:S(2)}) copy-start(f32[3,8192]{1,0:T(4,128)} %disp_far.1) | copy-start | bytes 294916
  1.4 68.7 %copy-start.7 = (f32[3,8192]{1,0:T(4,128)S(1)}, f32[3,8192]{1,0:T(4,128)}, u32[]{:S(2)}) copy-start(f32[3,8192]{1,0:T(4,128)} %vel_far.1) | copy-start | bytes 294916
  69.3 0.8 %copy-start.2 = (f32[24,24]{1,0:T(8,128)S(1)}, f32[24,24]{1,0:T(8,128)}, u32[]{:S(2)}) copy-start(f32[24,24]{1,0:T(8,128)} %stiff_far.1) | copy-start | bytes 6916

commit v4 on v3

--- a/solution.py
+++ b/solution.py
@@ -10,6 +10,7 @@
 NB = 128
 SUBSTEPS = 8
 LANES = 8
+FAR_FIRST = (4, 3, 5, 2, 6, 1, 7)
 OWN = 8
 DEPTH = 3
 NODE_ROWS = 16
@@ -74,8 +75,8 @@
     rim_out, rim_in, halo_out, halo_in,
     first_pay, first_a, first_b, pay, buf_a, buf_b, last_pay, last_a, last_b, react, disp_all,
     disp, vel, based, mass, contact, table, slot_cols, kron, tri,
-    wab, back, conn_idx, half, perm, end1, end2, modulus, level, held, state,
-    send_sem, recv_sem, pay_send, first_recv, a_recv, b_recv, load_sem, halo_send, halo_recv, last_recv,
+    wab, back, keep_rows, strict, conn_idx, half, perm, end1, end2, modulus, level, held, state,
+    send_sem, recv_sem, pay_send, first_recv, a_recv, b_recv, load_sem, halo_send, halo_recv, last_recv, vouch,
 ):
     r = lax.axis_index("region")
     lane = lax.axis_index("lane")
@@ -109,9 +110,19 @@
     def _(k):
         signal(peer_a(shifted(spot_a, k, size_a)))
 
-    @pl.loop(1, chips)
-    def _(k):
-        signal(peer_b(shifted(chip, k, chips)))
+    deep = min(chips, LANES)
+    wide = chips // deep
+
+    def along_x(k):
+        return peer_b(lax.rem(chip // deep + k, wide) * deep + lax.rem(chip, deep))
+
+    def along_z(k):
+        return peer_b((chip // deep) * deep + lax.rem(chip + k, deep))
+
+    for k in range(1, deep):
+        signal(along_z(k))
+    for k in range(1, wide):
+        signal(along_x(k))
 
     @pl.when(lane == 0)
     def _():
@@ -171,42 +182,40 @@
     ]
     pick = jnp.concatenate(picks, axis=0)
     conn_f = conn_in[...].astype(f32)
-    block_data = jnp.concatenate(
-        [modulus_in[...], level_row, window_row, jnp.zeros((NB - 18, 64), f32)], axis=0
-    )
-    chosen = sum(dot_t(pick, part) for part in split3(block_data))
+    picked = LANES * PACK + 2 * EDGE
+    tiled = jnp.concatenate([modulus_in[...]] * 8, axis=0)
+    chosen = sum(dot_t(pick, part) for part in split3(tiled))
+    chosen = jnp.where(
+        (iota((picked, NB), 0) & 7) == iota((picked, NB), 1) // 16, chosen, 0.0
+    )
+    grouped = jnp.sum(chosen.reshape(picked // 8, 8, NB), axis=1)
+    facts = jnp.concatenate(
+        [level_row, window_row, jnp.ones((1, 64), f32), jnp.zeros((5, 64), f32)], axis=0
+    ).astype(bf16)
     chosen_conn = dot(pick, conn_f.astype(bf16))
+    spot = iota((NB, 64), 0).astype(f32)
+
+    def lane_rows(k, start, offset):
+        key = jnp.where(rank_key[k : k + 1, :] >= 0.0, rank_key[k : k + 1, :] + start, -1.0)
+        found = dot_t(facts, onehot(spot == key))
+        return jnp.concatenate(
+            [found[0:1, :], found[1:2, :] + float(offset) * found[2:3, :], jnp.zeros((2, NB), f32)],
+            axis=0,
+        )
+
+    quarter = (PACK * lax.rem(lane, 4)).astype(f32)
+    eighth = (EDGE * lane).astype(f32)
     for k in range(LANES):
-        part = slice(k * PACK, (k + 1) * PACK)
-        pack_out[k, :, :NB] = chosen_conn[part, :]
-        pack_out[k, :, NB:] = chosen[part, :] + jnp.where(
-            iota((PACK, NB), 1) == 17, float(DEPTH - 1 - OWN * k), 0.0
+        pack_out[k, :PACK, :] = chosen_conn[k * PACK : (k + 1) * PACK, :]
+        pack_out[k, PACK : PACK + 4, :] = grouped[4 * k : 4 * k + 4, :]
+        pack_out[k, PACK + 4 :, :] = lane_rows(k, quarter, DEPTH - 1 - OWN * k)
+    for k, offset in ((0, DEPTH - 1 - OWN * LANES), (1, OWN + DEPTH - 1)):
+        start = LANES * PACK + k * EDGE
+        edge_out[k, :EDGE, :] = chosen_conn[start : start + EDGE, :]
+        edge_out[k, EDGE : EDGE + 4, :] = jnp.concatenate(
+            [grouped[start // 8 : start // 8 + 2, :], jnp.zeros((2, NB), f32)], axis=0
         )
-    for k, offset in ((0, DEPTH - 1 - OWN * LANES), (1, OWN + DEPTH - 1)):
-        part = slice(LANES * PACK + k * EDGE, LANES * PACK + (k + 1) * EDGE)
-        edge_out[k, :, :NB] = chosen_conn[part, :]
-        edge_out[k, :, NB:] = chosen[part, :] + jnp.where(
-            iota((EDGE, NB), 1) == 17, float(offset), 0.0
-        )
-
-    def load_rim(rim_lane, first):
-        for j in range(DEPTH):
-            at = (rim_lane * OWN + first + j) * NB
-            part = slice(at, at + NB)
-            for c in range(3):
-                rim_out[c, j : j + 1, :] = disp_in[c : c + 1, part]
-                rim_out[3 + c, j : j + 1, :] = vel_in[c : c + 1, part]
-        rows = slice(rim_lane * OWN + first, rim_lane * OWN + first + DEPTH)
-        rim_out[6, :, :] = mass_in[rows, :]
-        rim_out[7, :, :] = contact_in[rows, :]
-
-    @pl.when(lane == 0)
-    def _():
-        load_rim(LANES - 1, OWN - DEPTH)
-
-    @pl.when(lane == LANES - 1)
-    def _():
-        load_rim(0, 0)
+        edge_out[k, EDGE + 4 :, :] = lane_rows(LANES + k, eighth, offset)
 
     def load_nodes(place, source_lane, first, number):
         start = pl.multiple_of(source_lane * (OWN * NB), OWN * NB)
@@ -225,8 +234,6 @@
     mass[...] = jnp.ones_like(mass)
     contact[...] = jnp.zeros_like(contact)
     load_nodes(0, lane, 0, OWN)
-    load_nodes(left_row, jnp.maximum(lane - 1, 0), OWN - DEPTH, DEPTH)
-    load_nodes(right_row, jnp.minimum(lane + 1, LANES - 1), 0, DEPTH)
 
     own = pl.ds(0, OWN)
     own_contact = contact[own, :]
@@ -240,7 +247,11 @@
     first_pay[...] = jnp.concatenate(sums, axis=0)
     first_a[spot_a] = first_pay[...]
 
-    pl.semaphore_wait(pltpu.get_barrier_semaphore(), size_a - 1 + chips - 1 + 2)
+    pl.semaphore_wait(pltpu.get_barrier_semaphore(), size_a - 1 + deep - 1 + wide - 1 + 2)
+    for k in range(1, wide):
+        pl.semaphore_signal(
+            vouch, inc=1, device_id=along_x(k), device_id_type=pl.DeviceIdType.MESH
+        )
 
     @pl.loop(1, size_a)
     def _(k):
@@ -256,13 +267,31 @@
     edge_up.start()
     edge_down.start()
 
-    @pl.loop(1, LANES)
-    def _(k):
+    for k in FAR_FIRST:
         there = shifted(lane, k, LANES)
         copy(
             pack_out.at[there], pack_in.at[lane], send_sem.at[3], recv_sem.at[2], (r, there)
         ).start()
 
+    def load_rim(rim_lane, first):
+        for j in range(DEPTH):
+            at = (rim_lane * OWN + first + j) * NB
+            part = slice(at, at + NB)
+            for c in range(3):
+                rim_out[c, j : j + 1, :] = disp_in[c : c + 1, part]
+                rim_out[3 + c, j : j + 1, :] = vel_in[c : c + 1, part]
+        rows = slice(rim_lane * OWN + first, rim_lane * OWN + first + DEPTH)
+        rim_out[6, :, :] = mass_in[rows, :]
+        rim_out[7, :, :] = contact_in[rows, :]
+
+    @pl.when(lane == 0)
+    def _():
+        load_rim(LANES - 1, OWN - DEPTH)
+
+    @pl.when(lane == LANES - 1)
+    def _():
+        load_rim(0, 0)
+
     rim_up = copy(rim_out, rim_in, send_sem.at[2], recv_sem.at[1], (up, 0))
     rim_down = copy(rim_out, rim_in, send_sem.at[2], recv_sem.at[1], (down, LANES - 1))
 
@@ -275,6 +304,8 @@
         rim_down.start()
 
     pack_in[lane] = pack_out[lane]
+    load_nodes(left_row, jnp.maximum(lane - 1, 0), OWN - DEPTH, DEPTH)
+    load_nodes(right_row, jnp.minimum(lane + 1, LANES - 1), 0, DEPTH)
 
     lane64 = iota((64, NB), 1)
     keys = conn_f * float(NB) + lane64.astype(f32)
@@ -304,8 +335,7 @@
     order_up.start()
     order_down.start()
 
-    @pl.loop(1, LANES)
-    def _(k):
+    for k in FAR_FIRST:
         there = shifted(lane, k, LANES)
         copy(
             order_out.at[there], order_in.at[lane], send_sem.at[4], recv_sem.at[3], (r, there)
@@ -313,6 +343,8 @@
 
     order_in[lane] = order_out[lane]
 
+    offered = LANES * (PACK + EDGE)
+    strict[...] = onehot(iota((offered, offered), 0) < iota((offered, offered), 1))
     stiff = split2(stiff_in[...])
     at = iota((3 * NB, 24), 0)
     names = onehot((at // NB) * 8 + lax.rem(at, 8) == iota((3 * NB, 24), 1))
@@ -333,6 +365,8 @@
         edge_in[...] = jnp.zeros_like(edge_in)
         order_edge_in[...] = jnp.zeros_like(order_edge_in)
 
+    if wide > 1:
+        pl.semaphore_wait(vouch, wide - 1)
     wait_bytes(first_a.at[pl.ds(0, size_a - 1)], first_recv.at[0])
     total = first_a[0]
     for k in range(1, size_a):
@@ -369,31 +403,44 @@
 
     wait_bytes(pack_in.at[pl.ds(0, LANES - 1)], recv_sem.at[2])
 
-    offered = LANES * (PACK + EDGE)
-    rows_in = jnp.concatenate(
-        [pack_in[...].reshape(LANES * PACK, 2 * NB), edge_in[...].reshape(LANES * EDGE, 2 * NB)],
+    conn_rows = jnp.concatenate(
+        [pack_in[j, :PACK, :] for j in range(LANES)] + [edge_in[j, :EDGE, :] for j in range(LANES)],
         axis=0,
     )
-    data_in = rows_in[:, NB:]
-    data_parts = split3(data_in)
-    looked = onehot(iota((8, NB), 1) == 16)
-    present = jnp.where(dot_t(looked, data_parts[0]) > 0.0, 1.0, 0.0)
-    strict = onehot(iota((offered, offered), 0) < iota((offered, offered), 1))
-    key = jnp.where(present > 0.0, dot(present.astype(bf16), strict), -1.0)[0:1, :]
+    shared = jnp.concatenate(
+        [pack_in[j, PACK : PACK + 4, :] for j in range(LANES)]
+        + [edge_in[j, EDGE : EDGE + 2, :] for j in range(LANES)],
+        axis=0,
+    )
+    shared = jnp.broadcast_to(shared[:, None, :], (offered // 8, 8, NB)).reshape(offered, NB)
+    moduli = take(shared, 16 * (iota((offered, NB), 0) & 7) + iota((offered, NB), 1) // 8)
+    facts_in = jnp.concatenate(
+        [
+            sum(pack_in[j, PACK + 4 :, :] for j in range(4)),
+            sum(pack_in[j, PACK + 4 :, :] for j in range(4, LANES)),
+            sum(edge_in[j, EDGE + 4 :, :] for j in range(LANES)),
+        ],
+        axis=1,
+    )
+    levels_in = facts_in[0:1, :]
+    anchors_in = facts_in[1:2, :]
+    present = jnp.where(levels_in > 0.0, 1.0, 0.0) + jnp.zeros((8, offered), f32)
+    key = jnp.where(present > 0.0, dot(present.astype(bf16), strict[...]), -1.0)[0:1, :]
     taken = jnp.sum(present[0:1, :], axis=1, keepdims=True)
     overflow = jnp.maximum(overflow, jnp.where(taken > float(ROWS), 1.0, 0.0))
     keep = onehot(iota((ROWS, offered), 0).astype(f32) == key)
-    conn = dot(keep, rows_in[:, :NB].astype(bf16))
-    data = dot(keep, data_parts[0]) + dot(keep, data_parts[1]) + dot(keep, data_parts[2])
+    conn = dot(keep, conn_rows.astype(bf16))
+    moduli_parts = split3(moduli)
+    modulus[...] = sum(dot(keep, part) for part in moduli_parts)
+    wide_levels = (levels_in + jnp.zeros((NB, offered), f32)).astype(bf16)
+    wide_anchors = (anchors_in + jnp.zeros((NB, offered), f32)).astype(bf16)
 
     lane_no = iota((ROWS, NB), 1)
-    modulus[...] = take(data, lane_no // 8)
-    level[...] = take(data, jnp.full((ROWS, NB), 16, i32)).astype(i32) - 1
-    anchor = take(data, jnp.full((ROWS, NB), 17, i32)).astype(i32)
+    level[...] = dot_t(keep, wide_levels).astype(i32) - 1
+    anchor = dot_t(keep, wide_anchors).astype(i32)
     wab[:ROWS, :] = onehot((lane_no & 31) == row_of(anchor))
     wab[ROWS:, :] = onehot((lane_no & 31) == row_of(anchor + 1))
-    named = dot_t(onehot(iota((8, NB), 1) == 17), data.astype(bf16))
-    anchor_row = named[0:1, :].astype(i32)
+    anchor_row = dot_t(wide_anchors[:8, :], keep)[0:1, :].astype(i32)
     node_row = iota((NODE_ROWS, ROWS), 0)
     back_a = onehot(node_row == row_of(anchor_row))
     back_b = onehot(node_row == row_of(anchor_row + 1))
@@ -402,29 +449,7 @@
     conn_idx[...] = conn_i & (NB - 1)
     half[...] = conn_i >> 7
 
-    @pl.when((lane == 0) | (lane == LANES - 1))
-    def _():
-        wait_bytes(order_edge_in, recv_sem.at[6])
-
-    wait_bytes(order_in.at[pl.ds(0, LANES - 1)], recv_sem.at[3])
-    order_rows = jnp.concatenate(
-        [
-            order_in[...].reshape(LANES * PACK, NB),
-            order_edge_in[...].reshape(LANES * EDGE, NB),
-        ],
-        axis=0,
-    )
-    order = dot(keep, order_rows.astype(bf16)).astype(i32)
-    perm[...] = order
-    nodes = take(conn_i, order)
-    for ref, base in ((end1, 0), (end2, NB)):
-        target = lane_no + base
-        found = jnp.zeros((ROWS, NB), i32)
-        for step in (64, 32, 16, 8, 4, 2, 1, 0):
-            probe = take(nodes, found + (step - 1 if step else 0))
-            found = jnp.where(probe <= target, found + max(step, 1), found)
-        ref[...] = found - 1
-
+    keep_rows[...] = keep
     held[...] = jnp.zeros_like(held)
     table[...] = jnp.zeros_like(table)
 
@@ -467,19 +492,50 @@
             )
         return slots
 
+    def receive_order():
+        lane_no = iota((ROWS, NB), 1)
+
+        @pl.when((lane == 0) | (lane == LANES - 1))
+        def _():
+            wait_bytes(order_edge_in, recv_sem.at[6])
+
+        wait_bytes(order_in.at[pl.ds(0, LANES - 1)], recv_sem.at[3])
+        order_rows = jnp.concatenate(
+            [
+                order_in[...].reshape(LANES * PACK, NB),
+                order_edge_in[...].reshape(LANES * EDGE, NB),
+            ],
+            axis=0,
+        )
+        order = dot(keep_rows[...], order_rows.astype(bf16)).astype(i32)
+        perm[...] = order
+        nodes = take(half[...] * NB + conn_idx[...], order)
+        for ref, base in ((end1, 0), (end2, NB)):
+            target = lane_no + base
+            found = jnp.zeros((ROWS, NB), i32)
+            for step in (64, 32, 16, 8, 4, 2, 1, 0):
+                probe = take(nodes, found + (step - 1 if step else 0))
+                found = jnp.where(probe <= target, found + max(step, 1), found)
+            ref[...] = found - 1
+
     def forces(s):
         top, rest = split2(jnp.concatenate(to_slots([disp[c] for c in range(3)]), axis=1))
         strain = dot(jnp.concatenate([top, rest, top], axis=1), kron[...])
         active = (level[...] & s) == 0
-        order = perm[...]
         mod = modulus[...]
-        sorted_forces = []
         for c in range(3):
             g = strain[:, c * NB : (c + 1) * NB]
             fresh = mod * (g + hardening * g * g * g)
-            now = jnp.where(active, fresh, held[c])
-            held[c] = now
-            sorted_forces.append(jnp.concatenate(split2(take(now, order)), axis=1))
+            held[c] = jnp.where(active, fresh, held[c])
+
+        @pl.when(s == 0)
+        def _():
+            receive_order()
+
+        order = perm[...]
+        sorted_forces = []
+        for c in range(3):
+            sorted_forces.append(jnp.concatenate(split2(take(held[c], order)), axis=1))
         sums = dot(jnp.concatenate(sorted_forces, axis=0), tri[...])
         e1 = end1[...]
         e2 = end2[...]
@@ -700,8 +756,7 @@
             for c in range(3):
                 ref[c : c + 1, pl.ds(start + j * NB, NB)] = source[c, j : j + 1, :]
 
-        @pl.loop(1, LANES)
-        def _(k):
+        for k in FAR_FIRST:
             there = (r, shifted(lane, k, LANES))
             copy(
                 ref.at[:, own_part], ref.at[:, own_part], send_sem.at[5 + slot],
@@ -763,14 +818,16 @@
             jax.ShapeDtypeStruct((SUBSTEPS,), f32),
             jax.ShapeDtypeStruct((1,), i32),
         ),
-        in_specs=[pl.BlockSpec(memory_space=pl.ANY)] * 9,
+        in_specs=[pl.BlockSpec(memory_space=pltpu.HBM)] * 5
+        + [vmem]
+        + [pl.BlockSpec(memory_space=pltpu.HBM)] * 3,
         out_specs=[vmem] * 2 + [pl.BlockSpec(memory_space=pltpu.SMEM)] * 2,
         scratch_shapes=[
             V(init_disp.shape, f32), V(init_vel.shape, f32), V((LANES * OWN, NB), f32),
             V((LANES * OWN, NB), f32), V((16, 64), f32), V((24, 24), f32),
             V((1, 64), i32), V((1, 64), i32), V((64, NB), i32),
-            V((LANES, PACK, 2 * NB), f32), V((LANES, PACK, 2 * NB), f32),
-            V((2, EDGE, 2 * NB), f32), V((LANES, EDGE, 2 * NB), f32),
+            V((LANES, PACK + 8, NB), f32), V((LANES, PACK + 8, NB), f32),
+            V((2, EDGE + 8, NB), f32), V((LANES, EDGE + 8, NB), f32),
             V((LANES, PACK, NB), f32), V((LANES, PACK, NB), f32),
             V((2, EDGE, NB), f32), V((LANES, EDGE, NB), f32),
             V((8, DEPTH, NB), f32), V((8, DEPTH, NB), f32),
@@ -785,6 +842,8 @@
             V((NB, 5 * NB), bf16), V((4 * ROWS, 3 * NB), bf16),
             V((9 * NB, 3 * NB), bf16), V((2 * NB, NB), bf16),
             V((2 * ROWS, NB), bf16), V((NODE_ROWS, 4 * ROWS), bf16),
+            V((ROWS, LANES * (PACK + EDGE)), bf16),
+            V((LANES * (PACK + EDGE), LANES * (PACK + EDGE)), bf16),
             V((ROWS, NB), i32), V((ROWS, NB), i32), V((ROWS, NB), i32),
             V((ROWS, NB), i32), V((ROWS, NB), i32),
             V((ROWS, NB), f32), V((ROWS, NB), i32), V((3, ROWS, NB), f32), V((8, NB), f32),
@@ -793,7 +852,7 @@
             pltpu.SemaphoreType.DMA((SUBSTEPS,)), pltpu.SemaphoreType.DMA((SUBSTEPS,)),
             pltpu.SemaphoreType.DMA((9,)),
             pltpu.SemaphoreType.DMA((2, 2)), pltpu.SemaphoreType.DMA((2, 2)),
-            pltpu.SemaphoreType.DMA((2,)),
+            pltpu.SemaphoreType.DMA((2,)), pltpu.SemaphoreType.REGULAR,
         ],
         compiler_params=pltpu.CompilerParams(
             collective_id=0, has_side_effects=True, vmem_limit_bytes=48 * 1024 * 1024
@@ -804,6 +863,25 @@
         levels.reshape(1, -1), windows.reshape(1, -1), conn,
     )
     return (disp, vel, react), flag[0]
+
+
+def hand_over(disp_in, vel_in, react_in, disp_out, vel_out, react_out):
+    disp_out[...] = disp_in[...]
+    vel_out[...] = vel_in[...]
+    for s in range(SUBSTEPS):
+        react_out[s] = react_in[s]
+
+
+def finish(results):
+    vmem = pl.BlockSpec(memory_space=pltpu.VMEM)
+    smem = pl.BlockSpec(memory_space=pltpu.SMEM)
+    return pl.pallas_call(
+        hand_over,
+        out_shape=tuple(jax.ShapeDtypeStruct(x.shape, f32) for x in results),
+        in_specs=[vmem, vmem, smem],
+        out_specs=(vmem, vmem, smem),
+        name="hand_over",
+    )(*results)
 
 
 def sum_over(value, axis):
@@ -928,7 +1006,7 @@
 def on_device(*arguments):
     regions = lax.axis_size("region")
     fast, flag = run_cycle(regions, *arguments)
-    return lax.cond(flag == 0, lambda: fast, lambda: plain_cycle(*arguments))
+    return finish(lax.cond(flag == 0, lambda: fast, lambda: plain_cycle(*arguments)))
 
 
 def solution(mesh):

time: 72.4 us -> 68.1 us (0.941)
  Pallas kernels: 67.9 us -> 65.2 us
  local copies, waits for them, and re-layouts: 2.53 us -> 0.7 us
    pallas_call x1, Pallas kernels: 67.9 us -> 64 us  [run_cycle(): pl.pallas_call(functools.partial(cycle_kernel, regions), out_shape=(jax.S...]
    unnamed x21 -> x18, local copies, waits for them, and re-layouts: 2.53 us -> 0.7 us
    pallas_call x0 -> x1, Pallas kernels: none -> 1.27 us  [finish(): pl.pallas_call(hand_over, out_shape=tuple((jax.ShapeDtypeStruct(x.shape,...]
where the time goes in v4:
time: 68.1 us; the launch traced here: 67.8 us
  Pallas kernels  65.2 us (96%)
  between operations  1.64 us (2%)
  local copies, waits for them, and re-layouts  0.7 us (1%)
    pallas_call x1, Pallas kernels, run_cycle(): pl.pallas_call(functools.partial(cycle_kernel, regions), out_shape=(jax.S...  64 us

profile of v4, /device:TPU:1, one launch (start us, length us, event | category | flops | bytes accessed | tf_op | source)
XLA Modules:
  0.0 67.8 jit_solution(3926477100770229969)
XLA Ops:
  0.6 0.0 copy-start.8
  0.6 0.0 copy-start
  0.7 0.0 copy-start.1
  0.7 0.7 copy-done.8
  1.3 0.0 copy-done
  1.3 0.0 copy-done.1
  1.3 0.0 copy-start.3
  1.3 0.0 copy-start.4
  1.3 0.0 copy-start.5
  1.4 0.0 copy-start.6
  1.4 0.0 copy-start.7
  1.4 64.0 %crush_cycle.1 = (f32[3,8192]{1,0:T(4,128)S(1)}, f32[3,8192]{1,0:T(4,128)S(1)}, f32[8]{0:T(128)S(1)}, s32[1]{0:T(128)}) custom-call(f32[3,8192]{1,0:T(4,128)} %disp_far.1, f32[3,8192]{1,0:T(4,128)} %vel_far.1, f32[64,128]{1,0:T(8,128)} %bitcast.665, f32[64,128]{1,0:T(8,128)} %bitcast.664, f32[16,64]{1,0:T(8,128)S(1)} %bitcast.722, f32[24,24]{1,0:T(8,128)} %stiff_far.1, ...), custom_call_target="tpu_custom_call" | custom-call | tf_op jit(solution)/shard_map/crush_cycle/pallas_call | solution.py:813
  65.3 0.0 copy-start.2
  66.1 0.0 copy-done.3
  66.1 0.0 copy-done.4
  66.1 0.0 copy-done.5
  66.1 0.0 copy-done.6
  66.1 0.0 copy-done.7
  66.1 0.0 copy-done.2
  66.1 0.2 conditional.1
  66.4 1.3 %hand_over.1 = (f32[3,8192]{1,0:T(4,128)}, f32[3,8192]{1,0:T(4,128)}, f32[8]{0:T(128)}) custom-call(f32[3,8192]{1,0:T(4,128)S(1)} %get-tuple-element.1567.disp_in, f32[3,8192]{1,0:T(4,128)S(1)} %get-tuple-element.1568.vel_in, f32[8]{0:T(128)S(1)} %get-tuple-element.1569.react_in), custom_call_target="tpu_custom_call" | custom-call | tf_op jit(solution)/shard_map/hand_over/pallas_call | solution.py:878
Async XLA Ops:
  0.6 0.7 %copy-start.8 = (f32[64,16]{0,1:T(8,128)S(1)}, f32[64,16]{0,1:T(8,128)}, u32[]{:S(2)}) copy-start(f32[64,16]{0,1:T(8,128)} %param.100) | copy-start | bytes 12292
  0.6 0.7 %copy-start = (s32[64]{0:T(128)S(1)}, s32[64]{0:T(128)}, u32[]{:S(2)}) copy-start(s32[64]{0:T(128)} %param.102) | copy-start | bytes 772
  0.7 0.7 %copy-start.1 = (s32[64]{0:T(128)S(1)}, s32[64]{0:T(128)}, u32[]{:S(2)}) copy-start(s32[64]{0:T(128)} %param.103) | copy-start | bytes 772
  1.3 64.7 %copy-start.3 = (f32[8192]{0:T(1024)S(1)}, f32[8192]{0:T(1024)}, u32[]{:S(2)}) copy-start(f32[8192]{0:T(1024)} %param.99) | copy-start | bytes 98308
  1.3 64.7 %copy-start.4 = (s32[64,128]{1,0:T(8,128)S(1)}, s32[64,128]{1,0:T(8,128)}, u32[]{:S(2)}) copy-start(s32[64,128]{1,0:T(8,128)} %conn_far.1) | copy-start | bytes 98308
  1.3 64.7 %copy-start.5 = (f32[8192]{0:T(1024)S(1)}, f32[8192]{0:T(1024)}, u32[]{:S(2)}) copy-start(f32[8192]{0:T(1024)} %param.98) | copy-start | bytes 98308
  1.4 64.7 %copy-start.6 = (f32[3,8192]{1,0:T(4,128)S(1)}, f32[3,8192]{1,0:T(4,128)}, u32[]{:S(2)}) copy-start(f32[3,8192]{1,0:T(4,128)} %disp_far.1) | copy-start | bytes 294916
  1.4 64.7 %copy-start.7 = (f32[3,8192]{1,0:T(4,128)S(1)}, f32[3,8192]{1,0:T(4,128)}, u32[]{:S(2)}) copy-start(f32[3,8192]{1,0:T(4,128)} %vel_far.1) | copy-start | bytes 294916
  65.3 0.8 %copy-start.2 = (f32[24,24]{1,0:T(8,128)S(1)}, f32[24,24]{1,0:T(8,128)}, u32[]{:S(2)}) copy-start(f32[24,24]{1,0:T(8,128)} %stiff_far.1) | copy-start | bytes 6916

commit v5 on v4

--- a/solution.py
+++ b/solution.py
@@ -60,6 +60,14 @@
 
 def row_of(ext):
     return jnp.where(ext < DEPTH, ext + OWN, jnp.where(ext < DEPTH + OWN, ext - DEPTH, ext))
+
+
+def tree_sum(values):
+    values = list(values)
+    while len(values) > 1:
+        pairs = [a + b for a, b in zip(values[::2], values[1::2])]
+        values = pairs + values[len(pairs) * 2 :]
+    return values[0]
 
 
 def onehot(mask):
@@ -91,11 +99,33 @@
     node_total = regions * LANES * OWN * NB
     impactor_mass = impactor_ratio * node_total
 
-    def peer_a(k):
-        return (chip * 2 + lax.rem(k, 2), k // 2)
-
     def peer_b(k):
         return (k * 2 + core, lane)
+
+    deep = min(chips, LANES)
+    wide = chips // deep
+
+    def ring(step, size):
+        return min(step, size - step)
+
+    steps_a = sorted(
+        ((y, c) for y in range(LANES) for c in range(2) if y or c),
+        key=lambda step: (-ring(step[0], LANES), step),
+    )
+    steps_b = sorted(
+        ((x, z) for x in range(wide) for z in range(deep) if x or z),
+        key=lambda step: (-ring(step[0], wide) - ring(step[1], deep), step),
+    )
+
+    def members_a():
+        for y, c in steps_a:
+            yield (chip * 2 + lax.rem(core + c, 2), lax.rem(lane + y, LANES))
+
+    def members_b():
+        for x, z in steps_b:
+            yield peer_b(
+                lax.rem(chip // deep + x, wide) * deep + lax.rem(lax.rem(chip, deep) + z, deep)
+            )
 
     def signal(device):
         pl.semaphore_signal(
@@ -106,12 +136,8 @@
     def shifted(spot, step, size):
         return lax.rem(spot + step, size)
 
-    @pl.loop(1, size_a)
-    def _(k):
-        signal(peer_a(shifted(spot_a, k, size_a)))
-
-    deep = min(chips, LANES)
-    wide = chips // deep
+    for there in members_a():
+        signal(there)
 
     def along_x(k):
         return peer_b(lax.rem(chip // deep + k, wide) * deep + lax.rem(chip, deep))
@@ -253,11 +279,9 @@
             vouch, inc=1, device_id=along_x(k), device_id_type=pl.DeviceIdType.MESH
         )
 
-    @pl.loop(1, size_a)
-    def _(k):
+    for there in members_a():
         copy(
-            first_pay, first_a.at[spot_a], pay_send.at[0], first_recv.at[0],
-            peer_a(shifted(spot_a, k, size_a)),
+            first_pay, first_a.at[spot_a], pay_send.at[0], first_recv.at[0], there
         ).start()
 
     edge_up = copy(edge_out.at[0], edge_in.at[lane], send_sem.at[0], recv_sem.at[0], (up, 0))
@@ -368,17 +392,13 @@
     if wide > 1:
         pl.semaphore_wait(vouch, wide - 1)
     wait_bytes(first_a.at[pl.ds(0, size_a - 1)], first_recv.at[0])
-    total = first_a[0]
-    for k in range(1, size_a):
-        total = total + first_a[k]
+    total = tree_sum(first_a[k] for k in range(size_a))
     first_b[chip] = total
     first_pay2 = first_b.at[chip]
 
-    @pl.loop(1, chips)
-    def _(k):
+    for there in members_b():
         copy(
-            first_pay2, first_b.at[chip], pay_send.at[1], first_recv.at[1],
-            peer_b(shifted(chip, k, chips)),
+            first_pay2, first_b.at[chip], pay_send.at[1], first_recv.at[1], there
         ).start()
 
     @pl.when((lane == 0) | (lane == LANES - 1))
@@ -460,9 +480,7 @@
 
     def collect_first():
         wait_bytes(first_b.at[pl.ds(0, chips - 1)], first_recv.at[1])
-        total = first_b[0]
-        for k in range(1, chips):
-            total = total + first_b[k]
+        total = tree_sum(first_b[k] for k in range(chips))
         first = jnp.sum(total, axis=1, keepdims=True)
         reaction = first[0:1, :] + zero_row
         speed = start_speed - dt * contact_stiffness * reaction / impactor_mass
@@ -597,32 +615,24 @@
         last_pay[...] = jnp.concatenate(rows, axis=0)
         last_a[spot_a] = last_pay[...]
 
-        @pl.loop(1, size_a)
-        def _(k):
+        for there in members_a():
             copy(
-                last_pay, last_a.at[spot_a], pay_send.at[4], last_recv.at[0],
-                peer_a(shifted(spot_a, k, size_a)),
+                last_pay, last_a.at[spot_a], pay_send.at[4], last_recv.at[0], there
             ).start()
 
     def relay_last():
         wait_bytes(last_a.at[pl.ds(0, size_a - 1)], last_recv.at[0])
-        value = last_a[0]
-        for k in range(1, size_a):
-            value = value + last_a[k]
+        value = tree_sum(last_a[k] for k in range(size_a))
         last_b[chip] = value
 
-        @pl.loop(1, chips)
-        def _(k):
+        for there in members_b():
             copy(
-                last_b.at[chip], last_b.at[chip], pay_send.at[5], last_recv.at[1],
-                peer_b(shifted(chip, k, chips)),
+                last_b.at[chip], last_b.at[chip], pay_send.at[5], last_recv.at[1], there
             ).start()
 
     def collect_last():
         wait_bytes(last_b.at[pl.ds(0, chips - 1)], last_recv.at[1])
-        value = last_b[0]
-        for k in range(1, chips):
-            value = value + last_b[k]
+        value = tree_sum(last_b[k] for k in range(chips))
         total = jnp.sum(value, axis=1, keepdims=True) + jnp.zeros((4, NB), f32)
         shift = state[7:8, :] - state[6:7, :]
         cubic = total[0:1] + shift * (total[1:2] + shift * (total[2:3] + shift * total[3:4]))
@@ -633,23 +643,17 @@
 
     def relay(s):
         wait_bytes(buf_a.at[s, pl.ds(0, size_a - 1)], a_recv.at[s])
-        value = buf_a[s, 0]
-        for k in range(1, size_a):
-            value = value + buf_a[s, k]
+        value = tree_sum(buf_a[s, k] for k in range(size_a))
         buf_b[s, chip] = value
 
-        @pl.loop(1, chips)
-        def _(k):
+        for there in members_b():
             copy(
-                buf_b.at[s, chip], buf_b.at[s, chip], pay_send.at[3], b_recv.at[s],
-                peer_b(shifted(chip, k, chips)),
+                buf_b.at[s, chip], buf_b.at[s, chip], pay_send.at[3], b_recv.at[s], there
             ).start()
 
     def collect(s):
         wait_bytes(buf_b.at[s, pl.ds(0, chips - 1)], b_recv.at[s])
-        value = buf_b[s, 0]
-        for k in range(1, chips):
-            value = value + buf_b[s, k]
+        value = tree_sum(buf_b[s, k] for k in range(chips))
         total = jnp.sum(value, axis=1, keepdims=True) + zero_row
         before_z = state[0:1, :]
         now_z = state[1:2, :]
@@ -695,11 +699,9 @@
 
         @pl.when(s < ahead)
         def _():
-            @pl.loop(1, size_a)
-            def _(k):
+            for there in members_a():
                 copy(
-                    pay.at[s], buf_a.at[s, spot_a], pay_send.at[2], a_recv.at[s],
-                    peer_a(shifted(spot_a, k, size_a)),
+                    pay.at[s], buf_a.at[s, spot_a], pay_send.at[2], a_recv.at[s], there
                 ).start()
 
         @pl.when((s == 2) | (s == 5))
@@ -776,11 +778,13 @@
     wait_bytes(disp_all.at[:, other_parts], recv_sem.at[4])
     for s in range(SUBSTEPS - 1):
         react_out[s] = jnp.max(react[s : s + 1, :])
+    unfit = jnp.max(jnp.where(jnp.abs(react[: SUBSTEPS - 1, :]) < jnp.inf, 0, 1))
     wait_bytes(vel_out.at[:, other_parts], recv_sem.at[5])
     disp_out[...] = disp_all[...] + dt * vel_out[...]
     collect_last()
-    react_out[SUBSTEPS - 1] = jnp.max(react[SUBSTEPS - 1 :, :])
-    flag_out[0] = jnp.max(jnp.where(jnp.abs(react[...]) < jnp.inf, 0, 1))
+    last = jnp.max(react[SUBSTEPS - 1 :, :])
+    react_out[SUBSTEPS - 1] = last
+    flag_out[0] = jnp.maximum(unfit, jnp.where(jnp.abs(last) < jnp.inf, 0, 1))
 
     edge_up.wait_send()
     edge_down.wait_send()

time: 68.1 us -> 66.4 us (0.975)
  Pallas kernels: 65.2 us -> 63.5 us
    pallas_call x1, Pallas kernels: 64 us -> 62.2 us  [run_cycle(): pl.pallas_call(functools.partial(cycle_kernel, regions), out_shape=(jax.S...]
where the time goes in v5:
time: 66.4 us; the launch traced here: 66.1 us
  Pallas kernels  63.5 us (96%)
  between operations  1.64 us (2%)
  local copies, waits for them, and re-layouts  0.7 us (1%)
    pallas_call x1, Pallas kernels, run_cycle(): pl.pallas_call(functools.partial(cycle_kernel, regions), out_shape=(jax.S...  62.2 us

profile of v5, /device:TPU:1, one launch (start us, length us, event | category | flops | bytes accessed | tf_op | source)
XLA Modules:
  0.0 66.1 jit_solution(5602756416240268669)
XLA Ops:
  0.6 0.0 copy-start.8
  0.6 0.0 copy-start
  0.7 0.0 copy-start.1
  0.7 0.7 %copy-done.8 = f32[64,16]{0,1:T(8,128)S(1)} copy-done((f32[64,16]{0,1:T(8,128)S(1)}, f32[64,16]{0,1:T(8,128)}, u32[]{:S(2)}) %copy-start.8) | copy-done | bytes 4120
  1.3 0.0 copy-done
  1.3 0.0 copy-done.1
  1.3 0.0 copy-start.3
  1.3 0.0 copy-start.4
  1.3 0.0 copy-start.5
  1.4 0.0 copy-start.6
  1.4 0.0 copy-start.7
  1.4 62.2 %crush_cycle.1 = (f32[3,8192]{1,0:T(4,128)S(1)}, f32[3,8192]{1,0:T(4,128)S(1)}, f32[8]{0:T(128)S(1)}, s32[1]{0:T(128)}) custom-call(f32[3,8192]{1,0:T(4,128)} %disp_far.1, f32[3,8192]{1,0:T(4,128)} %vel_far.1, f32[64,128]{1,0:T(8,128)} %bitcast.665, f32[64,128]{1,0:T(8,128)} %bitcast.664, f32[16,64]{1,0:T(8,128)S(1)} %bitcast.722, f32[24,24]{1,0:T(8,128)} %stiff_far.1, ...), custom_call_target="tpu_custom_call" | custom-call | tf_op jit(solution)/shard_map/crush_cycle/pallas_call | solution.py:817
  63.6 0.0 copy-start.2
  64.3 0.0 copy-done.3
  64.4 0.0 copy-done.4
  64.4 0.0 copy-done.5
  64.4 0.0 copy-done.6
  64.4 0.0 copy-done.7
  64.4 0.0 copy-done.2
  64.4 0.2 conditional.1
  64.6 1.3 %hand_over.1 = (f32[3,8192]{1,0:T(4,128)}, f32[3,8192]{1,0:T(4,128)}, f32[8]{0:T(128)}) custom-call(f32[3,8192]{1,0:T(4,128)S(1)} %get-tuple-element.1567.disp_in, f32[3,8192]{1,0:T(4,128)S(1)} %get-tuple-element.1568.vel_in, f32[8]{0:T(128)S(1)} %get-tuple-element.1569.react_in), custom_call_target="tpu_custom_call" | custom-call | tf_op jit(solution)/shard_map/hand_over/pallas_call | solution.py:882
Async XLA Ops:
  0.6 0.7 %copy-start.8 = (f32[64,16]{0,1:T(8,128)S(1)}, f32[64,16]{0,1:T(8,128)}, u32[]{:S(2)}) copy-start(f32[64,16]{0,1:T(8,128)} %param.100) | copy-start | bytes 12292
  0.6 0.7 %copy-start = (s32[64]{0:T(128)S(1)}, s32[64]{0:T(128)}, u32[]{:S(2)}) copy-start(s32[64]{0:T(128)} %param.102) | copy-start | bytes 772
  0.7 0.7 %copy-start.1 = (s32[64]{0:T(128)S(1)}, s32[64]{0:T(128)}, u32[]{:S(2)}) copy-start(s32[64]{0:T(128)} %param.103) | copy-start | bytes 772
  1.3 63.0 %copy-start.3 = (f32[8192]{0:T(1024)S(1)}, f32[8192]{0:T(1024)}, u32[]{:S(2)}) copy-start(f32[8192]{0:T(1024)} %param.99) | copy-start | bytes 98308
  1.3 63.0 %copy-start.4 = (s32[64,128]{1,0:T(8,128)S(1)}, s32[64,128]{1,0:T(8,128)}, u32[]{:S(2)}) copy-start(s32[64,128]{1,0:T(8,128)} %conn_far.1) | copy-start | bytes 98308
  1.3 63.0 %copy-start.5 = (f32[8192]{0:T(1024)S(1)}, f32[8192]{0:T(1024)}, u32[]{:S(2)}) copy-start(f32[8192]{0:T(1024)} %param.98) | copy-start | bytes 98308
  1.4 63.0 %copy-start.6 = (f32[3,8192]{1,0:T(4,128)S(1)}, f32[3,8192]{1,0:T(4,128)}, u32[]{:S(2)}) copy-start(f32[3,8192]{1,0:T(4,128)} %disp_far.1) | copy-start | bytes 294916
  1.4 63.0 %copy-start.7 = (f32[3,8192]{1,0:T(4,128)S(1)}, f32[3,8192]{1,0:T(4,128)}, u32[]{:S(2)}) copy-start(f32[3,8192]{1,0:T(4,128)} %vel_far.1) | copy-start | bytes 294916
  63.6 0.8 %copy-start.2 = (f32[24,24]{1,0:T(8,128)S(1)}, f32[24,24]{1,0:T(8,128)}, u32[]{:S(2)}) copy-start(f32[24,24]{1,0:T(8,128)} %stiff_far.1) | copy-start | bytes 6916

commit v6 on v5

--- a/solution.py
+++ b/solution.py
@@ -279,17 +279,16 @@
             vouch, inc=1, device_id=along_x(k), device_id_type=pl.DeviceIdType.MESH
         )
 
+    edge_up = copy(edge_out.at[0], edge_in.at[lane], send_sem.at[0], recv_sem.at[0], (up, 0))
+    edge_down = copy(
+        edge_out.at[1], edge_in.at[lane], send_sem.at[1], recv_sem.at[0], (down, LANES - 1)
+    )
+    edge_up.start()
+    edge_down.start()
     for there in members_a():
         copy(
             first_pay, first_a.at[spot_a], pay_send.at[0], first_recv.at[0], there
         ).start()
-
-    edge_up = copy(edge_out.at[0], edge_in.at[lane], send_sem.at[0], recv_sem.at[0], (up, 0))
-    edge_down = copy(
-        edge_out.at[1], edge_in.at[lane], send_sem.at[1], recv_sem.at[0], (down, LANES - 1)
-    )
-    edge_up.start()
-    edge_down.start()
 
     for k in FAR_FIRST:
         there = shifted(lane, k, LANES)

time: 66.4 us -> 66.4 us (level)
  no operation moved by 1% of the time
where the time goes in v6:
time: 66.4 us; the launch traced here: 66.2 us
  Pallas kernels  63.6 us (96%)
  between operations  1.64 us (2%)
  local copies, waits for them, and re-layouts  0.7 us (1%)
    pallas_call x1, Pallas kernels, run_cycle(): pl.pallas_call(functools.partial(cycle_kernel, regions), out_shape=(jax.S...  62.3 us

profile of v6, /device:TPU:1, one launch (start us, length us, event | category | flops | bytes accessed | tf_op | source)
XLA Modules:
  0.0 66.2 jit_solution(11778388967041259602)
XLA Ops:
  0.6 0.0 copy-start.8
  0.6 0.0 copy-start
  0.7 0.0 copy-start.1
  0.7 0.7 %copy-done.8 = f32[64,16]{0,1:T(8,128)S(1)} copy-done((f32[64,16]{0,1:T(8,128)S(1)}, f32[64,16]{0,1:T(8,128)}, u32[]{:S(2)}) %copy-start.8) | copy-done | bytes 4120
  1.3 0.0 copy-done
  1.3 0.0 copy-done.1
  1.3 0.0 copy-start.3
  1.3 0.0 copy-start.4
  1.3 0.0 copy-start.5
  1.4 0.0 copy-start.6
  1.4 0.0 copy-start.7
  1.4 62.3 %crush_cycle.1 = (f32[3,8192]{1,0:T(4,128)S(1)}, f32[3,8192]{1,0:T(4,128)S(1)}, f32[8]{0:T(128)S(1)}, s32[1]{0:T(128)}) custom-call(f32[3,8192]{1,0:T(4,128)} %disp_far.1, f32[3,8192]{1,0:T(4,128)} %vel_far.1, f32[64,128]{1,0:T(8,128)} %bitcast.665, f32[64,128]{1,0:T(8,128)} %bitcast.664, f32[16,64]{1,0:T(8,128)S(1)} %bitcast.722, f32[24,24]{1,0:T(8,128)} %stiff_far.1, ...), custom_call_target="tpu_custom_call" | custom-call | tf_op jit(solution)/shard_map/crush_cycle/pallas_call | solution.py:816
  63.7 0.0 copy-start.2
  64.4 0.0 copy-done.3
  64.4 0.0 copy-done.4
  64.4 0.0 copy-done.5
  64.4 0.0 copy-done.6
  64.4 0.0 copy-done.7
  64.4 0.0 copy-done.2
  64.5 0.2 conditional.1
  64.7 1.3 %hand_over.1 = (f32[3,8192]{1,0:T(4,128)}, f32[3,8192]{1,0:T(4,128)}, f32[8]{0:T(128)}) custom-call(f32[3,8192]{1,0:T(4,128)S(1)} %get-tuple-element.1567.disp_in, f32[3,8192]{1,0:T(4,128)S(1)} %get-tuple-element.1568.vel_in, f32[8]{0:T(128)S(1)} %get-tuple-element.1569.react_in), custom_call_target="tpu_custom_call" | custom-call | tf_op jit(solution)/shard_map/hand_over/pallas_call | solution.py:881
Async XLA Ops:
  0.6 0.7 %copy-start.8 = (f32[64,16]{0,1:T(8,128)S(1)}, f32[64,16]{0,1:T(8,128)}, u32[]{:S(2)}) copy-start(f32[64,16]{0,1:T(8,128)} %param.100) | copy-start | bytes 12292
  0.6 0.7 %copy-start = (s32[64]{0:T(128)S(1)}, s32[64]{0:T(128)}, u32[]{:S(2)}) copy-start(s32[64]{0:T(128)} %param.102) | copy-start | bytes 772
  0.7 0.7 %copy-start.1 = (s32[64]{0:T(128)S(1)}, s32[64]{0:T(128)}, u32[]{:S(2)}) copy-start(s32[64]{0:T(128)} %param.103) | copy-start | bytes 772
  1.3 63.1 %copy-start.3 = (f32[8192]{0:T(1024)S(1)}, f32[8192]{0:T(1024)}, u32[]{:S(2)}) copy-start(f32[8192]{0:T(1024)} %param.99) | copy-start | bytes 98308
  1.3 63.1 %copy-start.4 = (s32[64,128]{1,0:T(8,128)S(1)}, s32[64,128]{1,0:T(8,128)}, u32[]{:S(2)}) copy-start(s32[64,128]{1,0:T(8,128)} %conn_far.1) | copy-start | bytes 98308
  1.3 63.1 %copy-start.5 = (f32[8192]{0:T(1024)S(1)}, f32[8192]{0:T(1024)}, u32[]{:S(2)}) copy-start(f32[8192]{0:T(1024)} %param.98) | copy-start | bytes 98308
  1.4 63.1 %copy-start.6 = (f32[3,8192]{1,0:T(4,128)S(1)}, f32[3,8192]{1,0:T(4,128)}, u32[]{:S(2)}) copy-start(f32[3,8192]{1,0:T(4,128)} %disp_far.1) | copy-start | bytes 294916
  1.4 63.1 %copy-start.7 = (f32[3,8192]{1,0:T(4,128)S(1)}, f32[3,8192]{1,0:T(4,128)}, u32[]{:S(2)}) copy-start(f32[3,8192]{1,0:T(4,128)} %vel_far.1) | copy-start | bytes 294916
  63.7 0.8 %copy-start.2 = (f32[24,24]{1,0:T(8,128)S(1)}, f32[24,24]{1,0:T(8,128)}, u32[]{:S(2)}) copy-start(f32[24,24]{1,0:T(8,128)} %stiff_far.1) | copy-start | bytes 6916
